TPU v7x, 256 devices: a whole 4x4x8 slice. The times are simulated.
256 devices in a mesh: group: 16 (over y_hi, x, core), tensor: 16 (over z, y_lo).
Axes of the slice: x: 4, y: 4 (y_hi: 2, y_lo: 2; y = y_hi * 2 + y_lo), z: 8, core: 2. Of those that a mesh axis runs over, the one named last changes fastest.
Arguments:
- states: bfloat16 [64, 4, 5120], P('group'), may hold values from -38 to 38
- input_gain: bfloat16 [5120], replicated, may hold values from 0.25 to 1.75
- post_gain: bfloat16 [5120], replicated, may hold values from 0.25 to 1.75
- norm_gains: float32 [2, 128], replicated, may hold values from 0.4 to 2.5
- query_weight: bfloat16 [5120, 4096], P(None, 'tensor'), may hold values from -0.078125 to 0.078125
- key_value_weight: bfloat16 [2, 5120, 512], P(None, 'tensor'), may hold values from -0.078125 to 0.078125
- output_weight: bfloat16 [4096, 5120], P('tensor'), may hold values from -0.09375 to 0.09375
- query_down: float32 [5120, 64], P('tensor', 'group'), may hold values from -0.078125 to 0.078125
- query_up: float32 [64, 4096], P('group', 'tensor'), may hold values from -0.24 to 0.24
- pair_down: float32 [2, 5120, 64], P(None, 'tensor', 'group'), may hold values from -0.078125 to 0.078125
- pair_up: float32 [2, 64, 512], P(None, 'group', 'tensor'), may hold values from -0.24 to 0.24
- output_down: float32 [4096, 64], P('tensor', 'group'), may hold values from -0.09375 to 0.09375
- output_up: float32 [64, 5120], P('group', 'tensor'), may hold values from -0.24 to 0.24
- cache_keys: bfloat16 [64, 4096, 512], P('group', 'tensor'), may hold values from -608 to 608
- cache_values: bfloat16 [64, 4096, 512], P('group', 'tensor'), may hold values from -6 to 6
- lengths: int32 [64], P('group'), may hold values from 1024 to 4092, as said below
Outputs:
- residual: bfloat16 [64, 4, 5120], P('group')
- normed: bfloat16 [64, 4, 5120], P('group')
Inputs may be any that keep to these rules, and one draw needn't show every extreme that they name: `lengths`: positions of a game at or beyond its length hold no prompt token.
All inputs are finite; a program needn't handle non-finite values.
Results may differ from a plain program's by a relative error of at most 0.006.
The roundings to bfloat16 on the way count: a program that leaves them out, or rounds other values in their place, can miss the bound.
Values may be sent and summed in bfloat16 or wider, within the bound.
No kernel may reach another device: no remote copies, remote signals or barrier semaphores. Data moves between devices by JAX's collectives and lax.ppermute only.
A program may use at most 64 MiB of HBM per device.

v0:
```python
import math

import jax
import jax.numpy as jnp
from jax import lax
from jax.sharding import PartitionSpec as P

HD = 128
QH = 32
KVH = 4


epsilon = 1e-06
lowrank_adapter_scale = 2.0
rope_theta = 1000000.0
masked_score = -1e30


def merged_2(array, axis, combine):
    everything = jax.tree.map(lambda part: lax.all_gather(part, axis), array)
    first = jax.tree.map(lambda part: part[0], everything)

    def lap(k, so_far):
        return combine(so_far, jax.tree.map(lambda part: part[k], everything))

    return lax.fori_loop(1, lax.axis_size(axis), lap, first)


def norm_rows(values):
    return values * lax.rsqrt(jnp.mean(values * values, axis=-1, keepdims=True) + epsilon)


def rope_tables(positions, head_size):
    half_size = head_size // 2
    inverse = rope_theta ** (-(jnp.arange(half_size, dtype=jnp.float32) * 2.0 / head_size))
    angles = positions.astype(jnp.float32)[..., None] * inverse
    return (jnp.cos(angles), jnp.sin(angles))


def rotate_half(values, cosine, sine_table):
    half_size = values.shape[-1] // 2
    first_half = values[..., :half_size]
    second_half = values[..., half_size:]
    return jnp.concatenate(
        [
            first_half * cosine - second_half * sine_table,
            second_half * cosine + first_half * sine_table,
        ],
        axis=-1,
    )


def merge_factors(frozen_weight_matrix, down_factor, up_factor):
    lowrank_update_term = jnp.dot(down_factor, up_factor, precision=lax.Precision.HIGHEST)
    return (
        frozen_weight_matrix.astype(jnp.float32) + lowrank_adapter_scale * lowrank_update_term
    ).astype(jnp.bfloat16)


def combine_partials(first_part, second_part):
    first_max, first_sum, first_acc = first_part
    second_max, latter_half_sum, second_acc = second_part
    highest = jnp.maximum(first_max, second_max)
    first_scaling = jnp.exp(first_max - highest)
    second_scaling = jnp.exp(second_max - highest)
    joint_sum = first_sum * first_scaling + latter_half_sum * second_scaling
    joint_acc = first_acc * first_scaling[..., None] + second_acc * second_scaling[..., None]
    return (highest, joint_sum, joint_acc)


def local(
    states,
    input_gain,
    post_gain,
    norm_gains,
    query_weight,
    key_value_weight,
    output_weight,
    query_down,
    query_up,
    pair_down,
    pair_up,
    output_down,
    output_up,
    cache_keys,
    cache_values,
    lengths,
):
    tensor_index = lax.axis_index("tensor")
    gathered = (
        lax.all_gather(query_down, "group", axis=1, tiled=True),
        lax.all_gather(query_up, "group", axis=0, tiled=True),
        lax.all_gather(pair_down, "group", axis=2, tiled=True),
        lax.all_gather(pair_up, "group", axis=1, tiled=True),
        lax.all_gather(output_down, "group", axis=1, tiled=True),
        lax.all_gather(output_up, "group", axis=0, tiled=True),
    )
    down_rows, query_up_own, pair_down_own, pair_up_part, output_down_own, output_up_part = gathered
    query_down_all, pair_up_all, output_up_all = (
        lax.all_gather(down_rows, "tensor", axis=0, tiled=True),
        lax.all_gather(pair_up_part, "tensor", axis=2, tiled=True),
        lax.all_gather(output_up_part, "tensor", axis=1, tiled=True),
    )
    query_merged = merge_factors(query_weight, query_down_all, query_up_own)
    key_value_update = jnp.einsum(
        "ndr,nrk->ndk", pair_down_own, pair_up_all, precision=lax.Precision.HIGHEST
    )
    key_value_combined = (
        key_value_weight.astype(jnp.float32) + lowrank_adapter_scale * key_value_update
    ).astype(jnp.bfloat16)
    output_merged = merge_factors(output_weight, output_down_own, output_up_all)
    game_count, step_count, model_width = states.shape
    local_heads = query_weight.shape[1] // HD
    share_count = QH // KVH
    score_scale = 1.0 / math.sqrt(HD)
    activations = states.astype(jnp.float32)
    normed_input = (norm_rows(activations) * input_gain.astype(jnp.float32)).astype(jnp.bfloat16)
    row_width = key_value_weight.shape[1]
    input_rows = lax.dynamic_slice_in_dim(normed_input, tensor_index * row_width, row_width, 2)
    pair_part = jnp.einsum(
        "gsd,ndk->ngsk", input_rows, key_value_combined, preferred_element_type=jnp.float32
    )
    pair_summed = lax.psum(pair_part, "tensor")
    positions = lengths[:, None] + jnp.arange(step_count, dtype=jnp.int32)[None, :]
    cosine, sine_table = rope_tables(positions, HD)
    cosine_heads = cosine[:, :, None, :]
    sine_heads = sine_table[:, :, None, :]
    key_raw = pair_summed[0].reshape(game_count, step_count, KVH, HD)
    fresh_keys = rotate_half(norm_rows(key_raw) * norm_gains[1], cosine_heads, sine_heads).astype(
        jnp.bfloat16
    )
    fresh_values = pair_summed[1].reshape(game_count, step_count, KVH, HD).astype(jnp.bfloat16)
    query_raw = jnp.einsum(
        "gsd,dc->gsc", normed_input, query_merged, preferred_element_type=jnp.float32
    )
    query_raw = query_raw.reshape(game_count, step_count, local_heads, HD)
    query_own = rotate_half(norm_rows(query_raw) * norm_gains[0], cosine_heads, sine_heads).astype(
        jnp.bfloat16
    )
    query_all = lax.all_gather(
        query_own.reshape(game_count, step_count, local_heads * HD), "tensor", axis=2, tiled=True
    )
    query_all = query_all.reshape(game_count, step_count, KVH, share_count, HD)
    block_size = cache_keys.shape[1]
    block_keys = cache_keys.reshape(game_count, block_size, KVH, HD)
    block_values = cache_values.reshape(game_count, block_size, KVH, HD)
    scores = (
        jnp.einsum("gskqd,gbkd->gskqb", query_all, block_keys, preferred_element_type=jnp.float32)
        * score_scale
    )
    slot_index = tensor_index * block_size + jnp.arange(block_size, dtype=jnp.int32)
    valid_mask = (slot_index[None, :] < lengths[:, None])[:, None, None, None, :]
    masked = jnp.where(valid_mask, scores, masked_score)
    block_running_peak = jnp.max(masked, axis=-1)
    block_weights = jnp.where(valid_mask, jnp.exp(masked - block_running_peak[..., None]), 0.0)
    block_sum = jnp.sum(block_weights, axis=-1)
    block_acc = jnp.einsum(
        "gskqb,gbkd->gskqd",
        block_weights.astype(jnp.bfloat16),
        block_values,
        preferred_element_type=jnp.float32,
    )
    block_running_peak = block_running_peak.reshape(game_count, step_count, QH)
    block_sum = block_sum.reshape(game_count, step_count, QH)
    block_acc = block_acc.reshape(game_count, step_count, QH, HD)
    merged = merged_2((block_running_peak, block_sum, block_acc), "tensor", combine_partials)
    own_max = lax.dynamic_slice_in_dim(merged[0], tensor_index * local_heads, local_heads, 2)
    own_sum = lax.dynamic_slice_in_dim(merged[1], tensor_index * local_heads, local_heads, 2)
    own_acc = lax.dynamic_slice_in_dim(merged[2], tensor_index * local_heads, local_heads, 2)
    pair_index = tensor_index * local_heads // share_count
    own_keys = lax.dynamic_slice_in_dim(fresh_keys, pair_index, 1, 2)[:, :, 0]
    own_values = lax.dynamic_slice_in_dim(fresh_values, pair_index, 1, 2)[:, :, 0]
    fresh_scores = (
        jnp.einsum("gshd,gtd->gsht", query_own, own_keys, preferred_element_type=jnp.float32)
        * score_scale
    )
    causal = (jnp.arange(step_count)[:, None] >= jnp.arange(step_count)[None, :])[None, :, None, :]
    fresh_masked = jnp.where(causal, fresh_scores, masked_score)
    fresh_max = jnp.max(fresh_masked, axis=-1)
    fresh_weights = jnp.where(causal, jnp.exp(fresh_masked - fresh_max[..., None]), 0.0)
    fresh_sum = jnp.sum(fresh_weights, axis=-1)
    fresh_acc = jnp.einsum(
        "gsht,gtd->gshd",
        fresh_weights.astype(jnp.bfloat16),
        own_values,
        preferred_element_type=jnp.float32,
    )
    joint_max, joint_sum, joint_acc = combine_partials(
        (own_max, own_sum, own_acc), (fresh_max, fresh_sum, fresh_acc)
    )
    attended = (
        (joint_acc / joint_sum[..., None])
        .astype(jnp.bfloat16)
        .reshape(game_count * step_count, local_heads * HD)
    )
    row_total = game_count * step_count
    flat_states = activations.reshape(row_total, model_width)
    projected = lax.psum(
        jnp.dot(attended, output_merged, preferred_element_type=jnp.float32), "tensor"
    )
    stream = flat_states + projected
    residual_out = stream.astype(jnp.bfloat16)
    normed_out = (norm_rows(stream) * post_gain.astype(jnp.float32)).astype(jnp.bfloat16)
    return (
        residual_out.reshape(game_count, step_count, model_width),
        normed_out.reshape(game_count, step_count, model_width),
    )


def solution(mesh):
    in_specs = (
        P("group", None, None),
        P(),
        P(),
        P(),
        P(None, "tensor"),
        P(None, "tensor", None),
        P("tensor", None),
        P("tensor", "group"),
        P("group", "tensor"),
        P(None, "tensor", "group"),
        P(None, "group", "tensor"),
        P("tensor", "group"),
        P("group", "tensor"),
        P("group", "tensor", None),
        P("group", "tensor", None),
        P("group"),
    )
    out_specs = (P("group", None, None), P("group", None, None))
    return jax.shard_map(local, mesh=mesh, in_specs=in_specs, out_specs=out_specs, check_vma=False)
```

profile of v0, /device:TPU:8, one launch (start us, length us, event | category | flops | bytes accessed | tf_op | source)
XLA Modules:
  0.0 588.0 jit_solution(8129931073040989814)
XLA Ops:
  7.3 24.1 %all-gather = f32[16,4,320]{2,1,0:T(4,128)S(1)} all-gather(f32[1,4,320]{2,1,0:T(4,128)} %bitcast.107), channel_id=1, replica_groups=mesh['group'=16,'tensor'=16] {'group'}, dimensions={0}, use_global_device_ids=true | all-gather | bytes 87040 | tf_op jit(solution)/shard_map/all_gather | solution.py:91
  33.5 19.5 %all_gather.47 = f32[2,64,32]{2,0,1:T(2,128)S(1)} all-gather(f32[2,4,32]{2,0,1:T(2,128)S(1)} %copy.106), channel_id=1, replica_groups=mesh['group'=16,'tensor'=16] {'group'}, dimensions={1}, use_global_device_ids=true | all-gather | bytes 17408 | tf_op jit(solution)/shard_map/all_gather | solution.py:94
  53.7 21.5 %all_gather.46 = f32[2,320,64]{1,0,2:T(2,128)S(1)} all-gather(f32[2,320,4]{1,0,2:T(2,128)S(1)} %copy.105), channel_id=1, replica_groups=mesh['group'=16,'tensor'=16] {'group'}, dimensions={2}, use_global_device_ids=true | all-gather | bytes 174080 | tf_op jit(solution)/shard_map/all_gather | solution.py:93
  75.2 37.6 %all_gather.48 = f32[2,64,512]{1,0,2:T(2,128)S(1)} all-gather(f32[2,64,32]{1,0,2:T(2,128)S(1)} %copy.107), channel_id=1, replica_groups=mesh['group'=16,'tensor'=16] {'tensor'}, dimensions={2}, use_global_device_ids=true | all-gather | bytes 278528 | tf_op jit(solution)/shard_map/all_gather | solution.py:101
  113.9 2.5 fusion.10
  117.5 21.6 %all-gather.4 = f32[16,4,320]{2,1,0:T(4,128)S(1)} all-gather(f32[1,4,320]{2,1,0:T(4,128)S(1)} %bitcast.108), channel_id=1, replica_groups=mesh['group'=16,'tensor'=16] {'group'}, dimensions={0}, use_global_device_ids=true | all-gather | bytes 87040 | tf_op jit(solution)/shard_map/all_gather | solution.py:96
  140.1 19.4 %all-gather.2 = f32[16,4,256]{2,1,0:T(4,128)S(1)} all-gather(f32[1,4,256]{2,1,0:T(4,128)S(1)} %bitcast.109), channel_id=1, replica_groups=mesh['group'=16,'tensor'=16] {'group'}, dimensions={0}, use_global_device_ids=true | all-gather | bytes 69632 | tf_op jit(solution)/shard_map/all_gather | solution.py:92
  162.0 2.3 copy.92
  164.8 5.9 %fusion.7 = bf16[5120,256,1]{1,0,2:T(8,128)(2,1)S(1)} fusion(f32[5120,64]{0,1:T(8,128)S(1)} %reshape.154, f32[64,256]{1,0:T(8,128)S(1)} %reshape.156, bf16[5120,256]{1,0:T(8,128)(2,1)} %param.22), kind=kOutput, calls=%fused_computation.14 | convolution fusion | flops 1011875840 | bytes 6619136 | tf_op jit(solution)/shard_map/dot_general | solution.py:54
  171.8 33.9 %all_gather.42 = bf16[4,4,4096]{2,1,0:T(4,128)(2,1)S(1)} all-gather(bf16[4,4,256]{2,1,0:T(4,128)(2,1)S(1)} %fusion.66), channel_id=1, replica_groups=mesh['group'=16,'tensor'=16] {'tensor'}, dimensions={2}, use_global_device_ids=true | all-gather | bytes 139264 | tf_op jit(solution)/shard_map/all_gather | solution.py:140
  207.5 20.6 %all-gather.3 = f32[16,4,256]{2,1,0:T(4,128)S(1)} all-gather(f32[1,4,256]{2,1,0:T(4,128)S(1)} %bitcast.110), channel_id=1, replica_groups=mesh['group'=16,'tensor'=16] {'group'}, dimensions={0}, use_global_device_ids=true | all-gather | bytes 69632 | tf_op jit(solution)/shard_map/all_gather | solution.py:95
  228.2 16.9 %all-reduce.3.cloned.1.call-done = f32[2,4,4,512]{3,2,1,0:T(4,128)} async-done(((f32[2,4,4,512]{3,2,1,0:T(4,128)}), f32[2,4,4,512]{3,2,1,0:T(4,128)}) %all-reduce.3.cloned.1.call-update) | async-done | bytes 65552 | tf_op jit(solution)/shard_map/psum | solution.py:123
  247.6 68.4 %all-gather.14.cloned.1.call-done = f32[16,320,64]{1,2,0:T(8,128)} async-done(((f32[1,320,64]{1,2,0:T(8,128)}), f32[16,320,64]{1,2,0:T(8,128)}) %all-gather.14.cloned.1.call-update) | async-done | bytes 1310736 | tf_op jit(solution)/shard_map/all_gather | solution.py:102
  316.1 2.3 copy.116
  318.4 1.5 reshape.162
  319.9 31.7 %all_gather.44 = f32[16,4,4,32]{3,2,1,0:T(4,128)S(1)} all-gather(f32[1,4,4,32]{3,2,1,0:T(4,128)S(1)} %all_gather_reshape.10), channel_id=1, replica_groups=mesh['group'=16,'tensor'=16] {'tensor'}, dimensions={0}, use_global_device_ids=true | all-gather | bytes 34816 | tf_op jit(solution)/shard_map/all_gather | solution.py:20
  351.7 34.0 %all_gather.43 = f32[16,4,4,32]{3,2,1,0:T(4,128)S(1)} all-gather(f32[1,4,4,32]{3,2,1,0:T(4,128)S(1)} %all_gather_reshape.9), channel_id=1, replica_groups=mesh['group'=16,'tensor'=16] {'tensor'}, dimensions={0}, use_global_device_ids=true | all-gather | bytes 34816 | tf_op jit(solution)/shard_map/all_gather | solution.py:20
  386.0 6.5 %fusion.6 = bf16[256,5120]{1,0:T(8,128)(2,1)S(1)} fusion(f32[64,256]{1,0:T(8,128)S(1)} %reshape.158, f32[5120,64]{0,1:T(8,128)} %reshape.162, bf16[256,5120]{1,0:T(8,128)(2,1)} %param.24), kind=kOutput, calls=%fused_computation.13 | convolution fusion | flops 1011875840 | bytes 6619136 | tf_op jit(solution)/shard_map/dot_general | solution.py:54
  392.4 28.2 %all-gather.10.cloned.1.call-done = f32[16,4,4,32,128]{4,3,2,1,0:T(8,128)} async-done(((f32[1,4,4,32,128]{4,3,2,1,0:T(8,128)}), f32[16,4,4,32,128]{4,3,2,1,0:T(8,128)}) %all-gather.10.cloned.1.call-update) | async-done | bytes 4194320 | tf_op jit(solution)/shard_map/all_gather | solution.py:20
  421.6 19.1 %while.19 = (s32[]{:T(128)}, f32[4,4,32]{2,1,0:T(4,128)S(1)}, f32[4,4,32]{2,1,0:T(4,128)S(1)}, f32[4,4,32,128]{3,2,1,0:T(8,128)S(1)}, f32[16,4,4,32]{3,2,1,0:T(4...) while((s32[]{:T(128)}, f32[4,4,32]{2,1,0:T(4,128)S(1)}, ...), condition=%wide.region_5.6_spmd, body=%wide.region_4.5_spmd.sunk | while | flops 199685 | bytes 807063 | solution.py:26
  421.7 1.2 fusion.70
  422.9 1.2 fusion.70
  424.2 1.2 fusion.70
  425.5 1.2 fusion.70
  426.7 1.2 fusion.70
  428.0 1.2 fusion.70
  429.3 1.2 fusion.70
  430.5 1.2 fusion.70
  431.8 1.2 fusion.70
  433.1 1.2 fusion.70
  436.9 1.2 fusion.70
  442.6 136.2 %all-reduce.5.cloned.1.call-done = f32[16,5120]{1,0:T(8,128)} async-done(((f32[16,5120]{1,0:T(8,128)}), f32[16,5120]{1,0:T(8,128)}) %all-reduce.5.cloned.1.call-update) | async-done | bytes 327696 | tf_op jit(solution)/shard_map/psum | solution.py:198
  (121 shorter events, 25.5 us)
Async XLA Ops:
  7.2 109.2 %copy-start.1 = (bf16[4,4,5120]{2,1,0:T(4,128)(2,1)S(1)}, bf16[4,4,5120]{2,1,0:T(4,128)(2,1)}, u32[]{:S(2)}) copy-start(bf16[4,4,5120]{2,1,0:T(4,128)(2,1)} %param.18) | copy-start | bytes 491524
  7.2 110.4 %copy-start.6 = (f32[4,320]{1,0:T(4,128)S(1)}, f32[4,320]{1,0:T(4,128)}, u32[]{:S(2)}) copy-start(f32[4,320]{1,0:T(4,128)} %param.30) | copy-start | bytes 15364
  7.2 132.8 %copy-start.10 = (f32[2,128]{1,0:T(2,128)S(1)}, f32[2,128]{1,0:T(2,128)}, u32[]{:S(2)}) copy-start(f32[2,128]{1,0:T(2,128)} %param.21) | copy-start | bytes 3076
  7.2 132.8 %copy-start.9 = (s32[4]{0:T(128)S(1)}, s32[4]{0:T(128)}, u32[]{:S(2)}) copy-start(s32[4]{0:T(128)} %param.33) | copy-start | bytes 52
  7.2 132.9 %copy-start.7 = (f32[4,256]{1,0:T(4,128)S(1)}, f32[4,256]{1,0:T(4,128)}, u32[]{:S(2)}) copy-start(f32[4,256]{1,0:T(4,128)} %param.26) | copy-start | bytes 12292
  7.2 154.8 %all-gather.12.cloned.1.call-start = ((), (), s32[]{:S(2)}) async-start(), calls=%async_computation.3 | async-start | bytes 1671168 | tf_op jit(solution)/shard_map/all_gather | solution.py:100
  31.3 128.3 %copy-start.2 = (bf16[4,256,512]{2,1,0:T(8,128)(2,1)S(1)}, bf16[4,256,512]{2,1,0:T(8,128)(2,1)}, u32[]{:S(2)}) copy-start(bf16[4,256,512]{2,1,0:T(8,128)(2,1)} %param.31) | copy-start | bytes 3145732
  32.0 213.1 %all-reduce.3.cloned.1.call-start = ((), (), s32[]{:S(2)}) async-start(), calls=%async_computation.1 | async-start | bytes 131072 | tf_op jit(solution)/shard_map/psum | solution.py:123
  113.9 46.8 %copy-start.3 = (bf16[4,256,512]{2,1,0:T(8,128)(2,1)S(1)}, bf16[4,256,512]{2,1,0:T(8,128)(2,1)}, u32[]{:S(2)}) copy-start(bf16[4,256,512]{2,1,0:T(8,128)(2,1)} %param.32) | copy-start | bytes 3145732
  117.5 198.6 %all-gather.14.cloned.1.call-start = ((), (), s32[]{:S(2)}) async-start(), calls=%async_computation.4 | async-start | bytes 1671168 | tf_op jit(solution)/shard_map/all_gather | solution.py:102
  139.9 280.7 %all-gather.10.cloned.1.call-start = ((), (), s32[]{:S(2)}) async-start(), calls=%async_computation | async-start | bytes 4456448 | tf_op jit(solution)/shard_map/all_gather | solution.py:20
  170.8 35.1 %copy-start = (bf16[4,256,4,128]{3,2,1,0:T(4,128)(2,1)S(1)}, bf16[4,256,4,128]{3,2,1,0:T(4,128)(2,1)}, u32[]{:S(2)}) copy-start(bf16[4,256,4,128]{3,2,1,0:T(4,128)(2,1)} %reshape.146) | copy-start | bytes 3145732
  170.8 35.6 %copy-start.4 = (bf16[4,256,4,128]{3,2,1,0:T(4,128)(2,1)S(1)}, bf16[4,256,4,128]{3,2,1,0:T(4,128)(2,1)}, u32[]{:S(2)}) copy-start(bf16[4,256,4,128]{3,2,1,0:T(4,128)(2,1)} %reshape.147) | copy-start | bytes 3145732
  171.3 36.3 %copy-start.8 = (f32[256,4]{0,1:T(4,128)S(1)}, f32[256,4]{0,1:T(4,128)}, u32[]{:S(2)}) copy-start(f32[256,4]{0,1:T(4,128)} %param.29) | copy-start | bytes 12292
  207.5 371.3 %all-reduce.5.cloned.1.call-start = ((), (), s32[]{:S(2)}) async-start(), calls=%async_computation.2 | async-start | bytes 655360 | tf_op jit(solution)/shard_map/psum | solution.py:198
  440.7 1.9 copy-start.5
Sparse Core Ops, SparseCore 0:
  32.1 70.4 all-gather.11
  117.6 127.4 all-reduce.2
  247.6 68.4 all-gather.13
  317.8 102.7 all-gather.9
  442.7 136.0 all-reduce.4
where the time goes:
time: 589 us; the launch traced here: 588 us
  blocking collectives  264 us (45%)
  waiting for transfers between devices  250 us (42%)
  other arithmetic  23.2 us (4%)
  matrix products  18.7 us (3%)
  local copies, waits for them, and re-layouts  17.6 us (3%)
  between operations  14.2 us (2%)
    psum x1, waiting for transfers between devices, local(): lax.psum(jnp.dot(attended, output_merged, preferred_element_type=jnp.floa...  136 us
    all_gather x1, waiting for transfers between devices, local(): lax.all_gather(output_up_part, 'tensor', axis=1, tiled=True)  68.4 us
    all_gather x2, blocking collectives, merged_2(): everything = jax.tree.map(lambda part: lax.all_gather(part, axis), array)  65.7 us
    all_gather x1, blocking collectives, local(): lax.all_gather(pair_up_part, 'tensor', axis=2, tiled=True)  37.6 us
    all_gather x1, blocking collectives, local(): lax.all_gather(query_own.reshape(game_count, step_count, local_heads * HD...  33.9 us
    all_gather x1, waiting for transfers between devices, merged_2(): everything = jax.tree.map(lambda part: lax.all_gather(part, axis), array)  28.2 us
    all_gather x1, blocking collectives, local(): lax.all_gather(query_down, 'group', axis=1, tiled=True)  24.1 us
    all_gather x1, blocking collectives, local(): lax.all_gather(output_up, 'group', axis=0, tiled=True)  21.6 us
  transfers between devices with their start and end apart: 5, of which 4 were waited for; matrix products, arithmetic and copies ran while one was open for 6% of the time, Pallas kernels for 0%

commit v1 on v0

v1 whole, which is shorter than its diff:
```python
import functools
import math

import jax
import jax.numpy as jnp
from jax import lax
from jax.experimental import pallas as pl
from jax.experimental.pallas import tpu as pltpu
from jax.sharding import PartitionSpec as P

HD = 128
QH = 32
KVH = 4
N = 16
ROWS = 16
GAMES = 4
STEPS = 4
RANK = 64
D = 5120
COLS = D // N
WIDE = COLS + RANK
BLOCK = 256

epsilon = 1e-06
rope_theta = 1000000.0
masked_score = -1e30
score_scale = 1.0 / math.sqrt(HD)
HIGHEST = lax.Precision.HIGHEST
f32 = jnp.float32
bf16 = jnp.bfloat16

VMEM = pl.BlockSpec(memory_space=pltpu.VMEM)
SMEM = pl.BlockSpec(memory_space=pltpu.SMEM)


def dot(a, b, contract=((1,), (0,)), precision=None):
    return lax.dot_general(
        a, b, (contract, ((), ())), precision=precision, preferred_element_type=f32
    )


def run(body, outs, args, name, specs=None, scratch=(), flops=0):
    return pl.pallas_call(
        body,
        out_shape=outs,
        in_specs=specs or [VMEM] * len(args),
        out_specs=jax.tree.map(lambda _: VMEM, outs),
        scratch_shapes=list(scratch),
        compiler_params=pltpu.CompilerParams(vmem_limit_bytes=48 << 20),
        name=name,
    )(*args)


def pack_factors(qd, qu, pd, pu, od, ou, out):
    block = jnp.concatenate(
        [
            jnp.concatenate([qd[...], pu[0], pu[1]], axis=1),
            jnp.concatenate([pd[0], jnp.zeros((4, 64), f32)], axis=1),
            jnp.concatenate([pd[1], jnp.zeros((4, 64), f32)], axis=1),
            jnp.concatenate([ou[...], jnp.zeros((4, 64), f32)], axis=1),
            jnp.concatenate([qu[...], jnp.zeros((4, 128), f32)], axis=1),
            jnp.concatenate([od[...], jnp.zeros((4, 128), f32)], axis=1),
        ],
        axis=0,
    )
    for g in range(N):
        out[g] = block


def own_columns(ref, t, rows):
    odd = lax.rem(t, 2)
    start = pl.multiple_of(t * COLS - odd * 64, 128)
    window = ref[:, pl.ds(start, WIDE)]
    return jnp.where(odd == 1, window[:, 64:WIDE], window[:, 0:COLS])


def normalise_input(
    recv, states, gain, kvw, out, x_out, st_out, qu_out, od_out, ou_out, act, xs, ranks, part
):
    t = lax.axis_index("tensor")
    for g in range(GAMES):
        act[4 * g : 4 * g + 4, :] = states[g].astype(f32)
    values = act[...]
    scale = lax.rsqrt(jnp.mean(values * values, axis=-1, keepdims=True) + epsilon)
    x = (values * scale * gain[...]).astype(bf16)
    x_out[...] = x
    xs[...] = x.astype(f32)
    st_out[...] = own_columns(act, t, ROWS)
    xt = own_columns(xs, t, ROWS)
    for g in range(N):
        for j in range(6):
            ranks[j, 4 * g : 4 * g + 4, :] = recv[g, 4 * j : 4 * j + 4, :]
    ou_out[...] = ranks[3, :, 0:COLS]
    qu_out[...] = ranks[4, :, 0:256]
    od_out[...] = ranks[5, :, 0:256]
    xb = xt.astype(bf16)
    for n in range(2):
        base = dot(xb, kvw[n])
        low = dot(xt, ranks[1 + n, :, 0:COLS], ((1,), (1,)), HIGHEST)
        part[:, 512 * n : 512 * n + 512] = base
        part[:, 1024 + 64 * n : 1088 + 64 * n] = low
    shared = ranks[0]
    for d in range(N):
        k, g = d // 4, d % 4
        rows = slice(4 * g, 4 * g + 4)
        out[d, 0:RANK, :] = shared
        out[d, RANK : RANK + 4, 0:128] = part[rows, 128 * k : 128 * k + 128]
        out[d, RANK : RANK + 4, 128:256] = part[rows, 512 + 128 * k : 640 + 128 * k]
        out[d, RANK : RANK + 4, 256:384] = part[rows, 1024:1152]
        out[d, RANK + 4 : RANK + 8, :] = jnp.zeros((4, WIDE), f32)


def rotate(values, cosine, sine):
    return values * cosine + pltpu.roll(values, HD // 2, 1) * sine


def head_norm(values, gain):
    return values * lax.rsqrt(jnp.mean(values * values, axis=-1, keepdims=True) + epsilon) * gain


def merge_queries(recv, qw, x, qu, gains, cos, sin, cos4, sin4, out, fk_out, fv_out):
    t = lax.axis_index("tensor")
    up = qu[...]
    raw = jnp.zeros((ROWS, 256), f32)
    for p in range(N // 2):
        merged = []
        for s in (2 * p, 2 * p + 1):
            update = dot(recv[s, 0:RANK, 0:COLS], up, ((0,), (0,)), HIGHEST)
            merged.append(
                (qw[COLS * s : COLS * s + COLS, :].astype(f32) + 2.0 * update).astype(bf16)
            )
        raw += dot(x[:, 640 * p : 640 * p + 640], jnp.concatenate(merged, axis=0))
    heads = []
    for h in range(2):
        v = head_norm(raw[:, HD * h : HD * h + HD], gains[0:1, :])
        heads.append(rotate(v, cos[...], sin[...]))
    queries = jnp.concatenate(heads, axis=1).astype(bf16)
    for d in range(N):
        out[d] = queries
    total = recv[0, RANK : RANK + 8, :]
    for s in range(1, N):
        total += recv[s, RANK : RANK + 8, :]
    group = 4 * (t // 4)
    keys, values = [], []
    for j in range(4):
        ups = recv[group + j, 0:RANK, COLS:WIDE]
        keys.append(dot(total[:, 256:320], ups[:, 0:32], precision=HIGHEST))
        values.append(dot(total[:, 320:384], ups[:, 32:64], precision=HIGHEST))
    key_raw = total[:, 0:128] + 2.0 * jnp.concatenate(keys, axis=1)
    value_raw = total[:, 128:256] + 2.0 * jnp.concatenate(values, axis=1)
    game = lax.rem(t, 4)
    fk = rotate(head_norm(key_raw, gains[1:2, :]), cos4[game], sin4[game])
    fk_out[...] = fk
    fv_out[...] = value_raw


def attend(lengths, recv, ck, cv, fk, fv, out, qs, ms, ls, accs):
    t = lax.axis_index("tensor")
    row = lax.broadcasted_iota(jnp.int32, (128, 1), 0)
    row_game = lax.rem(row, 16) // 4
    row_step = lax.rem(row, 4)
    length = jnp.zeros((128, 1), jnp.int32)
    for g in range(GAMES):
        length = jnp.where(row_game == g, lengths[g], length)
    slot = t * BLOCK + lax.broadcasted_iota(jnp.int32, (128, BLOCK), 1)
    valid = slot < length
    for k in range(KVH):
        q = jnp.concatenate(
            [recv[4 * k + i, :, HD * j : HD * j + HD] for i in range(4) for j in range(2)], axis=0
        )
        qs[k] = q
        lanes = slice(HD * k, HD * k + HD)
        scores = jnp.zeros((128, BLOCK), f32)
        for g in range(GAMES):
            own = dot(q, ck[g, :, lanes], ((1,), (1,)))
            scores = jnp.where(row_game == g, own, scores)
        scores = jnp.where(valid, scores * score_scale, masked_score)
        peak = jnp.max(scores, axis=-1, keepdims=True)
        weights = jnp.where(valid, jnp.exp(scores - peak), 0.0)
        ms[k] = peak
        ls[k] = jnp.sum(weights, axis=-1, keepdims=True)
        rounded = weights.astype(bf16)
        acc = jnp.zeros((128, HD), f32)
        for g in range(GAMES):
            mine = jnp.where(row_game == g, rounded, jnp.zeros_like(rounded))
            acc += dot(mine, cv[g, :, lanes])
        accs[k] = acc
    kk, game = t // 4, lax.rem(t, 4)
    zeros = jnp.zeros((120, HD), f32)
    keys = jnp.concatenate([fk[...], zeros], axis=0).astype(bf16)
    values = jnp.concatenate([fv[...], zeros], axis=0).astype(bf16)
    fresh = dot(qs[kk], keys, ((1,), (1,))) * score_scale
    later = lax.broadcasted_iota(jnp.int32, (128, 128), 1)
    causal = jnp.logical_and(row_game == game, later <= row_step)
    fresh = jnp.where(causal, fresh, masked_score)
    fresh_peak = jnp.max(fresh, axis=-1, keepdims=True)
    fresh_weights = jnp.where(causal, jnp.exp(fresh - fresh_peak), 0.0)
    fresh_sum = jnp.sum(fresh_weights, axis=-1, keepdims=True)
    fresh_acc = dot(fresh_weights.astype(bf16), values)
    highest = jnp.maximum(ms[kk], fresh_peak)
    old, new = jnp.exp(ms[kk] - highest), jnp.exp(fresh_peak - highest)
    ls[kk] = ls[kk] * old + fresh_sum * new
    accs[kk] = accs[kk] * old + fresh_acc * new
    ms[kk] = highest
    eye = lax.broadcasted_iota(jnp.int32, (128, 128), 0) == later
    for k in range(KVH):
        peaks = jnp.sum(jnp.where(eye, ms[k], 0.0), axis=0, keepdims=True)
        sums = jnp.sum(jnp.where(eye, ls[k], 0.0), axis=0, keepdims=True)
        for i in range(4):
            d = 4 * k + i
            out[d, 0:32, :] = accs[k, 32 * i : 32 * i + 32, :]
            shift = (128 - 32 * i) % 128
            a = pltpu.roll(peaks, shift, 1) if shift else peaks
            b = pltpu.roll(sums, shift, 1) if shift else sums
            out[d, 32:33, :] = a
            out[d, 33:34, :] = b
            out[d, 34:40, :] = jnp.zeros((6, 128), f32)


def project(recv, ow, od, out):
    peaks, sums = recv[:, 32, :], recv[:, 33, :]
    highest = jnp.max(peaks, axis=0, keepdims=True)
    scale = jnp.exp(peaks - highest)
    total = jnp.sum(sums * scale, axis=0, keepdims=True)
    share = scale / total
    share = jnp.concatenate([share, jnp.zeros((112, 128), f32)], axis=0).T
    acc = jnp.zeros((32, HD), f32)
    for s in range(N):
        acc += recv[s, 0:32, :] * share[0:32, s : s + 1]
    joint = jnp.concatenate([acc[0:16], acc[16:32]], axis=1)
    attended = joint.astype(bf16)
    low = dot(attended.astype(f32), od[...], ((1,), (1,)), HIGHEST)
    for p in range(N // 2):
        part = dot(attended, ow[:, 640 * p : 640 * p + 640])
        out[2 * p] = jnp.concatenate([part[:, 0:COLS], low], axis=1)
        out[2 * p + 1] = jnp.concatenate([part[:, COLS:640], low], axis=1)


def add_residual(recv, ou, st, out):
    total = recv[0]
    for s in range(1, N):
        total += recv[s]
    projected = total[:, 0:COLS] + 2.0 * dot(total[:, COLS:WIDE], ou[...], precision=HIGHEST)
    stream = st[...] + projected
    squares = jnp.sum(stream * stream, axis=-1, keepdims=True)
    high = squares.astype(bf16).astype(f32)
    middle = (squares - high).astype(bf16).astype(f32)
    low = squares - high - middle
    lane = lax.broadcasted_iota(jnp.int32, (ROWS, RANK), 1)
    tail = jnp.where(lane == 0, high, 0.0)
    tail = jnp.where(lane == 1, middle, tail)
    tail = jnp.where(lane == 2, low, tail)
    piece = jnp.concatenate([stream, tail], axis=1).astype(bf16)
    for d in range(N):
        out[d] = piece


def finish(recv, gain, residual, normed):
    squares = jnp.zeros((ROWS, RANK), f32)
    for s in range(N):
        squares += recv[s, :, COLS:WIDE].astype(f32)
    mean = jnp.sum(squares, axis=-1, keepdims=True) * (1.0 / D)
    scale = lax.rsqrt(mean + epsilon)
    for p in range(N // 2):
        lanes = slice(640 * p, 640 * p + 640)
        both = jnp.concatenate(
            [recv[2 * p, :, 0:COLS].astype(f32), recv[2 * p + 1, :, 0:COLS].astype(f32)], axis=1
        )
        scaled = both * scale * gain[:, lanes]
        for g in range(GAMES):
            rows = slice(4 * g, 4 * g + 4)
            residual[g, :, lanes] = both[rows].astype(bf16)
            normed[g, :, lanes] = scaled[rows].astype(bf16)


def exchange(array, axis):
    return lax.all_to_all(array, axis, 0, 0, tiled=True)


def rope_tables(lengths):
    positions = lengths[:, None] + jnp.arange(STEPS, dtype=jnp.int32)[None, :]
    inverse = rope_theta ** (-(jnp.arange(HD // 2, dtype=f32) * 2.0 / HD))
    angles = positions.astype(f32)[..., None] * inverse
    cos, sin = jnp.cos(angles), jnp.sin(angles)
    return jnp.concatenate([cos, cos], axis=-1), jnp.concatenate([-sin, sin], axis=-1)


def local(
    states,
    input_gain,
    post_gain,
    norm_gains,
    query_weight,
    key_value_weight,
    output_weight,
    query_down,
    query_up,
    pair_down,
    pair_up,
    output_down,
    output_up,
    cache_keys,
    cache_values,
    lengths,
):
    shape = jax.ShapeDtypeStruct
    cos, sin = rope_tables(lengths)
    factors = run(
        pack_factors,
        shape((N, 24, WIDE), f32),
        (
            query_down.T,
            query_up,
            pair_down.transpose(0, 2, 1),
            pair_up,
            output_down.T,
            output_up,
        ),
        "pack_factors",
    )
    factors = exchange(factors, "group")
    shared, x, own_states, up_query, down_output, up_output = run(
        normalise_input,
        (
            shape((N, RANK + 8, WIDE), f32),
            shape((ROWS, D), bf16),
            shape((ROWS, COLS), f32),
            shape((RANK, 256), f32),
            shape((RANK, 256), f32),
            shape((RANK, COLS), f32),
        ),
        (factors, states, input_gain.astype(f32)[None, :], key_value_weight),
        "normalise_input",
        scratch=[
            pltpu.VMEM((ROWS, D), f32),
            pltpu.VMEM((ROWS, D), f32),
            pltpu.VMEM((6, RANK, WIDE), f32),
            pltpu.VMEM((ROWS, 1152), f32),
        ],
    )
    shared = exchange(shared, "tensor")
    pad = jnp.zeros((GAMES, 4, HD), f32)
    queries, fresh_keys, fresh_values = run(
        merge_queries,
        (shape((N, ROWS, 256), bf16), shape((8, HD), f32), shape((8, HD), f32)),
        (
            shared,
            query_weight,
            x,
            up_query,
            norm_gains,
            cos.reshape(ROWS, HD),
            sin.reshape(ROWS, HD),
            jnp.concatenate([cos, pad], axis=1),
            jnp.concatenate([sin, pad], axis=1),
        ),
        "merge_queries",
    )
    queries = exchange(queries, "tensor")
    partials = run(
        attend,
        shape((N, 40, HD), f32),
        (lengths, queries, cache_keys, cache_values, fresh_keys, fresh_values),
        "attend",
        specs=[SMEM] + [VMEM] * 5,
        scratch=[
            pltpu.VMEM((KVH, 128, HD), bf16),
            pltpu.VMEM((KVH, 128, 1), f32),
            pltpu.VMEM((KVH, 128, 1), f32),
            pltpu.VMEM((KVH, 128, HD), f32),
        ],
    )
    partials = exchange(partials, "tensor")
    projected = run(
        project, shape((N, ROWS, WIDE), f32), (partials, output_weight, down_output), "project"
    )
    projected = exchange(projected, "tensor")
    pieces = run(
        add_residual,
        shape((N, ROWS, WIDE), bf16),
        (projected, up_output, own_states),
        "add_residual",
    )
    pieces = exchange(pieces, "tensor")
    return run(
        finish,
        (shape((GAMES, STEPS, D), bf16), shape((GAMES, STEPS, D), bf16)),
        (pieces, post_gain.astype(f32)[None, :]),
        "finish",
    )


def solution(mesh):
    in_specs = (
        P("group", None, None),
        P(),
        P(),
        P(),
        P(None, "tensor"),
        P(None, "tensor", None),
        P("tensor", None),
        P("tensor", "group"),
        P("group", "tensor"),
        P(None, "tensor", "group"),
        P(None, "group", "tensor"),
        P("tensor", "group"),
        P("group", "tensor"),
        P("group", "tensor", None),
        P("group", "tensor", None),
        P("group"),
    )
    out_specs = (P("group", None, None), P("group", None, None))
    return jax.shard_map(local, mesh=mesh, in_specs=in_specs, out_specs=out_specs, check_vma=False)
```

time: 589 us -> 153 us (0.26)
  blocking collectives: 264 us -> 43.5 us
  waiting for transfers between devices: 250 us -> 62.9 us
  other arithmetic: 23.2 us -> 1.22 us
  starting transfers between devices: 0.21 us -> 21 us
  matrix products: 18.7 us -> 0 us
  Pallas kernels: 0 us -> 14.1 us
  between operations: 14.2 us -> 0.74 us
  local copies, waits for them, and re-layouts: 17.6 us -> 8 us
    all_gather x10 -> x0, blocking collectives: 264 us -> none  [the longest x2 65.7 us: merged_2(): everything = jax.tree.map(lambda part: lax.all_gather(part, axis), array)]
    psum x2 -> x0, waiting for transfers between devices: 153 us -> none  [the longest x1 136 us: local(): lax.psum(jnp.dot(attended, output_merged, preferred_element_type=jnp.floa...]
    all_gather x3 -> x0, waiting for transfers between devices: 96.7 us -> none  [the longest x1 68.4 us: local(): lax.all_gather(output_up_part, 'tensor', axis=1, tiled=True)]
    all_to_all x0 -> x3, waiting for transfers between devices: none -> 62.9 us  [exchange(): return lax.all_to_all(array, axis, 0, 0, tiled=True)]
    all_to_all x0 -> x3, blocking collectives: none -> 43.5 us  [exchange(): return lax.all_to_all(array, axis, 0, 0, tiled=True)]
    all_to_all x0 -> x3, starting transfers between devices: none -> 21 us  [exchange(): return lax.all_to_all(array, axis, 0, 0, tiled=True)]
    dot_general x10 -> x0, matrix products: 18.7 us -> none  [the longest x2 12.4 us: merge_factors(): jnp.dot(down_factor, up_factor, precision=lax.Precision.HIGHEST)]
    add x32 -> x0, other arithmetic: 18.7 us -> none  [the longest x15 18.2 us: combine_partials(): first_acc * first_scaling[..., None]]
  transfers between devices with their start and end apart: 5 -> 3, of which waited for: 4 -> 3; matrix products, arithmetic and copies ran while one was open for 6% -> 1% of each run, Pallas kernels for 0% -> 0%
where the time goes in v1:
time: 153 us; the launch traced here: 151 us
  waiting for transfers between devices  62.9 us (41%)
  blocking collectives  43.5 us (28%)
  starting transfers between devices  21 us (14%)
  Pallas kernels  14.1 us (9%)
  local copies, waits for them, and re-layouts  8 us (5%)
    all_to_all x3, waiting for transfers between devices, exchange(): return lax.all_to_all(array, axis, 0, 0, tiled=True)  62.9 us
    all_to_all x3, blocking collectives, exchange(): return lax.all_to_all(array, axis, 0, 0, tiled=True)  43.5 us
    all_to_all x3, starting transfers between devices, exchange(): return lax.all_to_all(array, axis, 0, 0, tiled=True)  21 us
    pallas_call x7, Pallas kernels, run(): pl.pallas_call(body, out_shape=outs, in_specs=specs or [VMEM] * len(args)...  14.1 us
    unnamed x30, local copies, waits for them, and re-layouts  7.91 us
  transfers between devices with their start and end apart: 3, of which 3 were waited for; matrix products, arithmetic and copies ran while one was open for 1% of the time, Pallas kernels for 0%

profile of v1, /device:TPU:8, one launch (start us, length us, event | category | flops | bytes accessed | tf_op | source)
XLA Modules:
  0.0 151.5 jit_solution(3641636371666065483)
XLA Ops:
  0.6 0.7 copy-done.6
  1.3 0.7 copy-done.7
  2.0 0.7 copy-done.8
  2.7 0.7 copy-done.9
  3.4 0.7 copy-done.10
  4.1 0.7 copy-done.11
  4.8 0.9 pack_factors.1
  5.7 6.1 %all-to-all-start = ((f32[16,24,384]{2,1,0:T(8,128)}), f32[16,24,384]{2,1,0:T(8,128)S(1)}, u32[]{:S(2)}, u32[]{:S(2)}) async-start(f32[16,24,384]{2,1,0:T(8,128)} %pack_factors.1), calls=%async_computation | async-start | bytes 1179648 | tf_op jit(solution)/shard_map/all_to_all | solution.py:277
  11.9 0.7 broadcast_in_dim.19
  12.6 12.3 %all-to-all-done.recv = f32[16,24,384]{2,1,0:T(8,128)S(1)} async-done(((f32[16,24,384]{2,1,0:T(8,128)}), f32[16,24,384]{2,1,0:T(8,128)S(1)}, u32[]{:S(2)}, u32[]{:S(2)}) %all-to-all-start) | async-done | bytes 589856 | tf_op jit(solution)/shard_map/all_to_all | solution.py:277
  24.9 1.1 copy-done.4
  26.0 0.9 copy-done.5
  26.9 2.2 %normalise_input.1 = (f32[16,72,384]{2,1,0:T(8,128)}, bf16[16,5120]{1,0:T(8,128)(2,1)S(1)}, f32[16,320]{1,0:T(8,128)S(1)}, f32[64,256]{1,0:T(8,128)S(1)}, f32[64,256]{1,0:T(8,128)S(1)}, /*index=5*/f32[64,320]{1,0:T(8,128)S(1)}) custom-call(f32[16,24,384]{2,1,0:T(8,128)S(1)} %all-to-all-done.recv, bf16[4,4,5120]{2,1,0:T(4,128)(2,1)S(1)} %copy-done.5, ...), custom_call_target="tpu_custom_call" | custom-call | tf_op jit(solution)/shard_map/normalise_input/pallas_call | solution.py:43
  29.1 10.1 %all-to-all-start.1 = ((f32[16,72,384]{2,1,0:T(8,128)}), f32[16,72,384]{2,1,0:T(8,128)S(1)}, u32[]{:S(2)}, u32[]{:S(2)}) async-start(f32[16,72,384]{2,1,0:T(8,128)} %get-tuple-element.11), calls=%async_computation.1 | async-start | bytes 3538944 | tf_op jit(solution)/shard_map/all_to_all | solution.py:277
  39.2 0.1 add_convert_fusion
  39.2 0.1 convert_element_type.14
  39.3 0.1 fusion
  39.5 0.1 pad_maximum_fusion
  39.5 0.1 fusion.1
  39.7 0.1 select_maximum_fusion
  39.8 41.4 %all-to-all-done.1.recv = f32[16,72,384]{2,1,0:T(8,128)S(1)} async-done(((f32[16,72,384]{2,1,0:T(8,128)}), f32[16,72,384]{2,1,0:T(8,128)S(1)}, u32[]{:S(2)}, u32[]{:S(2)}) %all-to-all-start.1) | async-done | bytes 1769504 | tf_op jit(solution)/shard_map/all_to_all | solution.py:277
  81.2 1.7 %copy-done = bf16[5120,256]{1,0:T(8,128)(2,1)S(1)} copy-done((bf16[5120,256]{1,0:T(8,128)(2,1)S(1)}, bf16[5120,256]{1,0:T(8,128)(2,1)}, u32[]{:S(2)}) %copy-start) | copy-done | bytes 2621464
  83.0 5.4 %merge_queries.1 = (bf16[16,16,256]{2,1,0:T(8,128)(2,1)S(1)}, f32[8,128]{1,0:T(8,128)S(1)}, f32[8,128]{1,0:T(8,128)S(1)}) custom-call(f32[16,72,384]{2,1,0:T(8,128)S(1)} %all-to-all-done.1.recv, bf16[5120,256]{1,0:T(8,128)(2,1)S(1)} %copy-done, bf16[16,5120]{1,0:T(8,128)(2,1)S(1)} %get-tuple-element.12.x, f32[64,256]{1,0:T(8,128)S(1)} %get-tuple-element.13.qu, ...), custom_call_target="tpu_custom_call" | custom-call | tf_op jit(solution)/shard_map/merge_queries/pallas_call | solution.py:43
  88.4 13.2 %all_to_all.30.recv = bf16[16,16,256]{2,1,0:T(8,128)(2,1)S(1)} all-to-all(bf16[16,16,256]{2,1,0:T(8,128)(2,1)S(1)} %get-tuple-element.14), channel_id=1, replica_groups=mesh['group'=16,'tensor'=16] {'tensor'}, dimensions={0} | all-to-all | bytes 262144 | tf_op jit(solution)/shard_map/all_to_all | solution.py:277
  101.6 2.8 %attend.1 = f32[16,40,128]{2,1,0:T(8,128)S(1)} custom-call(s32[4]{0:T(128)S(1)} %copy-done.12, bf16[16,16,256]{2,1,0:T(8,128)(2,1)S(1)} %all_to_all.30.recv, bf16[4,256,512]{2,1,0:T(8,128)(2,1)S(1)} %copy-done.2, bf16[4,256,512]{2,1,0:T(8,128)(2,1)S(1)} %copy-done.3, f32[8,128]{1,0:T(8,128)S(1)} %get-tuple-element.15.fk, f32[8,128]{1,0:T(8,128)S(1)} %get-tuple-element.16.fv), custom_call_target="tpu_custom_call" | custom-call | tf_op jit(solution)/shard_map/attend/pallas_call | solution.py:43
  104.4 14.7 %all_to_all.31.recv = f32[16,40,128]{2,1,0:T(8,128)S(1)} all-to-all(f32[16,40,128]{2,1,0:T(8,128)S(1)} %attend.1), channel_id=1, replica_groups=mesh['group'=16,'tensor'=16] {'tensor'}, dimensions={0} | all-to-all | bytes 655360 | tf_op jit(solution)/shard_map/all_to_all | solution.py:277
  119.0 0.8 project.1
  119.9 15.7 %all_to_all.32.recv = f32[16,16,384]{2,1,0:T(8,128)S(1)} all-to-all(f32[16,16,384]{2,1,0:T(8,128)S(1)} %project.1), channel_id=1, replica_groups=mesh['group'=16,'tensor'=16] {'tensor'}, dimensions={0} | all-to-all | bytes 786432 | tf_op jit(solution)/shard_map/all_to_all | solution.py:277
  135.5 1.1 add_residual.1
  136.6 4.8 %all-to-all-start.5 = ((bf16[16,16,384]{2,1,0:T(8,128)(2,1)}), bf16[16,16,384]{2,1,0:T(8,128)(2,1)S(1)}, u32[]{:S(2)}, u32[]{:S(2)}) async-start(bf16[16,16,384]{2,1,0:T(8,128)(2,1)} %add_residual.1), calls=%async_computation.5 | async-start | bytes 393216 | tf_op jit(solution)/shard_map/all_to_all | solution.py:277
  141.4 9.1 %all-to-all-done.5.recv = bf16[16,16,384]{2,1,0:T(8,128)(2,1)S(1)} async-done(((bf16[16,16,384]{2,1,0:T(8,128)(2,1)}), bf16[16,16,384]{2,1,0:T(8,128)(2,1)S(1)}, u32[]{:S(2)}, u32[]{:S(2)}) %all-to-all-start.5) | async-done | bytes 196640 | tf_op jit(solution)/shard_map/all_to_all | solution.py:277
  150.5 0.9 finish.1
  (23 shorter events, 0.1 us)
Async XLA Ops:
  0.6 0.7 copy-start.6
  1.3 0.7 copy-start.7
  2.0 0.7 copy-start.8
  2.7 0.7 copy-start.9
  3.4 0.7 copy-start.10
  4.1 0.7 copy-start.11
  5.7 19.2 %all-to-all-start = ((f32[16,24,384]{2,1,0:T(8,128)}), f32[16,24,384]{2,1,0:T(8,128)S(1)}, u32[]{:S(2)}, u32[]{:S(2)}) async-start(f32[16,24,384]{2,1,0:T(8,128)} %pack_factors.1), calls=%async_computation | async-start | bytes 1179648 | tf_op jit(solution)/shard_map/all_to_all | solution.py:277
  11.9 27.3 %copy-start.12 = (s32[4]{0:T(128)S(1)}, s32[4]{0:T(128)}, u32[]{:S(2)}) copy-start(s32[4]{0:T(128)} %lengths.1) | copy-start | bytes 52
  11.9 69.3 %copy-start.13 = (f32[2,128]{1,0:T(2,128)S(1)}, f32[2,128]{1,0:T(2,128)}, u32[]{:S(2)}) copy-start(f32[2,128]{1,0:T(2,128)} %gains.1) | copy-start | bytes 3076
  24.9 1.1 copy-start.4
  26.0 0.9 copy-start.5
  29.1 72.5 %copy-start.2 = (bf16[4,256,512]{2,1,0:T(8,128)(2,1)S(1)}, bf16[4,256,512]{2,1,0:T(8,128)(2,1)}, u32[]{:S(2)}) copy-start(bf16[4,256,512]{2,1,0:T(8,128)(2,1)} %ck.1) | copy-start | bytes 3145732
  29.1 52.1 %all-to-all-start.1 = ((f32[16,72,384]{2,1,0:T(8,128)}), f32[16,72,384]{2,1,0:T(8,128)S(1)}, u32[]{:S(2)}, u32[]{:S(2)}) async-start(f32[16,72,384]{2,1,0:T(8,128)} %get-tuple-element.11), calls=%async_computation.1 | async-start | bytes 3538944 | tf_op jit(solution)/shard_map/all_to_all | solution.py:277
  81.2 1.7 %copy-start = (bf16[5120,256]{1,0:T(8,128)(2,1)S(1)}, bf16[5120,256]{1,0:T(8,128)(2,1)}, u32[]{:S(2)}) copy-start(bf16[5120,256]{1,0:T(8,128)(2,1)} %qw.1) | copy-start | bytes 7864324
  83.0 18.6 %copy-start.3 = (bf16[4,256,512]{2,1,0:T(8,128)(2,1)S(1)}, bf16[4,256,512]{2,1,0:T(8,128)(2,1)}, u32[]{:S(2)}) copy-start(bf16[4,256,512]{2,1,0:T(8,128)(2,1)} %cv.1) | copy-start | bytes 3145732
  88.4 30.6 %copy-start.1 = (bf16[256,5120]{1,0:T(8,128)(2,1)S(1)}, bf16[256,5120]{1,0:T(8,128)(2,1)}, u32[]{:S(2)}) copy-start(bf16[256,5120]{1,0:T(8,128)(2,1)} %ow.1) | copy-start | bytes 7864324
  119.0 22.4 %copy-start.14 = (bf16[5120]{0:T(1024)(128)(2,1)S(1)}, bf16[5120]{0:T(1024)(128)(2,1)}, u32[]{:S(2)}) copy-start(bf16[5120]{0:T(1024)(128)(2,1)} %param.18) | copy-start | bytes 30724
  136.6 13.9 %all-to-all-start.5 = ((bf16[16,16,384]{2,1,0:T(8,128)(2,1)}), bf16[16,16,384]{2,1,0:T(8,128)(2,1)S(1)}, u32[]{:S(2)}, u32[]{:S(2)}) async-start(bf16[16,16,384]{2,1,0:T(8,128)(2,1)} %add_residual.1), calls=%async_computation.5 | async-start | bytes 393216 | tf_op jit(solution)/shard_map/all_to_all | solution.py:277

commit v2 on v1

--- a/solution.py
+++ b/solution.py
@@ -31,6 +31,7 @@
 
 VMEM = pl.BlockSpec(memory_space=pltpu.VMEM)
 SMEM = pl.BlockSpec(memory_space=pltpu.SMEM)
+HBM = pl.BlockSpec(memory_space=pltpu.HBM)
 
 
 def dot(a, b, contract=((1,), (0,)), precision=None):
@@ -51,63 +52,73 @@
     )(*args)
 
 
-def pack_factors(qd, qu, pd, pu, od, ou, out):
-    block = jnp.concatenate(
-        [
-            jnp.concatenate([qd[...], pu[0], pu[1]], axis=1),
-            jnp.concatenate([pd[0], jnp.zeros((4, 64), f32)], axis=1),
-            jnp.concatenate([pd[1], jnp.zeros((4, 64), f32)], axis=1),
-            jnp.concatenate([ou[...], jnp.zeros((4, 64), f32)], axis=1),
-            jnp.concatenate([qu[...], jnp.zeros((4, 128), f32)], axis=1),
-            jnp.concatenate([od[...], jnp.zeros((4, 128), f32)], axis=1),
-        ],
-        axis=0,
-    )
-    for g in range(N):
-        out[g] = block
-
-
-def own_columns(ref, t, rows):
+def copies(pairs, sems):
+    started = [pltpu.make_async_copy(src, dst, sems.at[i]) for i, (src, dst) in enumerate(pairs)]
+    for copy in started:
+        copy.start()
+    return started
+
+
+def own_columns(ref, t):
     odd = lax.rem(t, 2)
     start = pl.multiple_of(t * COLS - odd * 64, 128)
     window = ref[:, pl.ds(start, WIDE)]
     return jnp.where(odd == 1, window[:, 64:WIDE], window[:, 0:COLS])
 
 
-def normalise_input(
-    recv, states, gain, kvw, out, x_out, st_out, qu_out, od_out, ou_out, act, xs, ranks, part
+def prepare(
+    qd_hbm, pu_hbm, states_hbm, kvw_hbm, gain, out, x_out, xt_out, st_out,
+    qd, pu, states, kvw, act, part, sems,
 ):
+    waits = copies(
+        [(states_hbm, states), (kvw_hbm, kvw), (qd_hbm, qd), (pu_hbm, pu)], sems
+    )
     t = lax.axis_index("tensor")
+    waits[0].wait()
     for g in range(GAMES):
         act[4 * g : 4 * g + 4, :] = states[g].astype(f32)
+    st_out[...] = own_columns(act, t)
     values = act[...]
     scale = lax.rsqrt(jnp.mean(values * values, axis=-1, keepdims=True) + epsilon)
     x = (values * scale * gain[...]).astype(bf16)
     x_out[...] = x
-    xs[...] = x.astype(f32)
-    st_out[...] = own_columns(act, t, ROWS)
-    xt = own_columns(xs, t, ROWS)
-    for g in range(N):
-        for j in range(6):
-            ranks[j, 4 * g : 4 * g + 4, :] = recv[g, 4 * j : 4 * j + 4, :]
-    ou_out[...] = ranks[3, :, 0:COLS]
-    qu_out[...] = ranks[4, :, 0:256]
-    od_out[...] = ranks[5, :, 0:256]
-    xb = xt.astype(bf16)
+    act[...] = x.astype(f32)
+    xt = own_columns(act, t)
+    xt_out[...] = xt
+    waits[1].wait()
     for n in range(2):
-        base = dot(xb, kvw[n])
-        low = dot(xt, ranks[1 + n, :, 0:COLS], ((1,), (1,)), HIGHEST)
-        part[:, 512 * n : 512 * n + 512] = base
-        part[:, 1024 + 64 * n : 1088 + 64 * n] = low
-    shared = ranks[0]
+        part[:, 512 * n : 512 * n + 512] = dot(xt.astype(bf16), kvw[n])
+    waits[2].wait()
+    waits[3].wait()
+    shared = jnp.concatenate([qd[...], pu[0], pu[1]], axis=1)
     for d in range(N):
         k, g = d // 4, d % 4
         rows = slice(4 * g, 4 * g + 4)
-        out[d, 0:RANK, :] = shared
-        out[d, RANK : RANK + 4, 0:128] = part[rows, 128 * k : 128 * k + 128]
-        out[d, RANK : RANK + 4, 128:256] = part[rows, 512 + 128 * k : 640 + 128 * k]
-        out[d, RANK : RANK + 4, 256:384] = part[rows, 1024:1152]
-        out[d, RANK + 4 : RANK + 8, :] = jnp.zeros((4, WIDE), f32)
+        out[d, 0:4, :] = shared
+        out[d, 4:8, 0:128] = part[rows, 128 * k : 128 * k + 128]
+        out[d, 4:8, 128:256] = part[rows, 512 + 128 * k : 640 + 128 * k]
+        out[d, 4:8, 256:384] = jnp.zeros((4, 128), f32)
+
+
+def regroup(recv, qu_hbm, pd_hbm, od_hbm, ou_hbm, out, base_out, qu, pd, od, ou, sems):
+    waits = copies([(qu_hbm, qu), (pd_hbm, pd), (od_hbm, od), (ou_hbm, ou)], sems)
+    t = lax.axis_index("tensor")
+    base = recv[0]
+    for s in range(1, N):
+        base += recv[s]
+    base_out[...] = base
+    for copy in waits:
+        copy.wait()
+    spare = [qu[:, 64 * c : 64 * c + 64] for c in range(4)]
+    spare += [od[:, 64 * c : 64 * c + 64] for c in range(4)]
+    spare += [ou[:, 64 * c : 64 * c + 64] for c in range(5)]
+    spare += [recv[4 * (t // 4) + c, 0:4, COLS:WIDE] for c in range(4)]
+    spare += [jnp.zeros((4, 64), f32)]
+    wide = [recv[b, 0:4, 0:COLS] for b in range(N)] + [pd[0], pd[1]]
+    blocks = [jnp.concatenate([w, s], axis=1) for w, s in zip(wide, spare)]
+    piece = jnp.concatenate(blocks, axis=0)
+    for d in range(N):
+        out[d] = piece
 
 
 def rotate(values, cosine, sine):
@@ -118,44 +129,76 @@
     return values * lax.rsqrt(jnp.mean(values * values, axis=-1, keepdims=True) + epsilon) * gain
 
 
-def merge_queries(recv, qw, x, qu, gains, cos, sin, cos4, sin4, out, fk_out, fv_out):
-    t = lax.axis_index("tensor")
-    up = qu[...]
+def split(values):
+    high = values.astype(bf16)
+    rest = values - high.astype(f32)
+    middle = rest.astype(bf16)
+    return high, middle, (rest - middle.astype(f32)).astype(bf16)
+
+
+def merge_queries(
+    recv, qw_hbm, x, xt, gains, cos, sin, out, od_out, ou_out, up_out, ranks, qw, sems
+):
+    chunks = N // 2
+    waits = copies(
+        [(qw_hbm.at[pl.ds(640 * p, 640)], qw.at[pl.ds(640 * p, 640)]) for p in range(chunks)], sems
+    )
+    for b in range(18):
+        for g in range(N):
+            ranks[b, 4 * g : 4 * g + 4, :] = recv[g, 4 * b : 4 * b + 4, :]
+    spare = [ranks[b, :, COLS:WIDE] for b in range(17)]
+    up = jnp.concatenate(spare[0:4], axis=1)
+    od_out[...] = jnp.concatenate(spare[4:8], axis=1)
+    ou_out[...] = jnp.concatenate(spare[8:13], axis=1)
+    for n in range(2):
+        up_out[n] = jnp.concatenate([c[:, 32 * n : 32 * n + 32] for c in spare[13:17]], axis=1)
+    uh, um, ul = split(up)
+    ups = jnp.concatenate([uh, uh, um, um, ul, uh], axis=0)
     raw = jnp.zeros((ROWS, 256), f32)
-    for p in range(N // 2):
+    for p in range(chunks):
+        waits[p].wait()
         merged = []
-        for s in (2 * p, 2 * p + 1):
-            update = dot(recv[s, 0:RANK, 0:COLS], up, ((0,), (0,)), HIGHEST)
-            merged.append(
-                (qw[COLS * s : COLS * s + COLS, :].astype(f32) + 2.0 * update).astype(bf16)
-            )
+        for b in (2 * p, 2 * p + 1):
+            h, m, l = split(ranks[b].T[0:COLS])
+            hm = jnp.concatenate([h, m], axis=1)
+            hl = jnp.concatenate([h, l], axis=1)
+            update = dot(jnp.concatenate([hm, hm, hl], axis=1), ups)
+            weight = qw[COLS * b : COLS * b + COLS, :].astype(f32)
+            merged.append((weight + 2.0 * update).astype(bf16))
         raw += dot(x[:, 640 * p : 640 * p + 640], jnp.concatenate(merged, axis=0))
     heads = []
     for h in range(2):
         v = head_norm(raw[:, HD * h : HD * h + HD], gains[0:1, :])
         heads.append(rotate(v, cos[...], sin[...]))
-    queries = jnp.concatenate(heads, axis=1).astype(bf16)
+    queries = jnp.concatenate(heads, axis=1).astype(bf16).astype(f32)
+    low = [
+        dot(xt[...], ranks[16 + n, :, 0:COLS], ((1,), (1,)), HIGHEST) for n in range(2)
+    ]
+    low = [part.astype(f32) for part in split(jnp.concatenate(low, axis=1))]
+    top = jnp.concatenate(low[0:2], axis=1)
+    bottom = jnp.concatenate([low[2], jnp.zeros((ROWS, 128), f32)], axis=1)
     for d in range(N):
-        out[d] = queries
-    total = recv[0, RANK : RANK + 8, :]
+        rows = slice(4 * (d % 4), 4 * (d % 4) + 4)
+        out[d] = jnp.concatenate([queries, top[rows], bottom[rows]], axis=0).astype(bf16)
+
+
+def fresh_pair(recv, base, up, gains, cos4, sin4, t):
+    total = recv[0, 16:24, :].astype(f32)
     for s in range(1, N):
-        total += recv[s, RANK : RANK + 8, :]
-    group = 4 * (t // 4)
-    keys, values = [], []
-    for j in range(4):
-        ups = recv[group + j, 0:RANK, COLS:WIDE]
-        keys.append(dot(total[:, 256:320], ups[:, 0:32], precision=HIGHEST))
-        values.append(dot(total[:, 320:384], ups[:, 32:64], precision=HIGHEST))
-    key_raw = total[:, 0:128] + 2.0 * jnp.concatenate(keys, axis=1)
-    value_raw = total[:, 128:256] + 2.0 * jnp.concatenate(values, axis=1)
+        total += recv[s, 16:24, :].astype(f32)
+    low = total[0:4, 0:128] + total[0:4, 128:256] + total[4:8, 0:128]
+    low = jnp.concatenate([low, jnp.zeros((4, 128), f32)], axis=0)
+    sums = jnp.concatenate([base[4:8, :], jnp.zeros((4, WIDE), f32)], axis=0)
+    keys = sums[:, 0:128] + 2.0 * dot(low[:, 0:64], up[0], precision=HIGHEST)
+    values = sums[:, 128:256] + 2.0 * dot(low[:, 64:128], up[1], precision=HIGHEST)
     game = lax.rem(t, 4)
-    fk = rotate(head_norm(key_raw, gains[1:2, :]), cos4[game], sin4[game])
-    fk_out[...] = fk
-    fv_out[...] = value_raw
-
-
-def attend(lengths, recv, ck, cv, fk, fv, out, qs, ms, ls, accs):
+    keys = rotate(head_norm(keys, gains[1:2, :]), cos4[game], sin4[game])
+    return keys, values
+
+
+def attend(lengths, recv, ck, cv, base, up, gains, cos4, sin4, out, qs, ms, ls, accs):
     t = lax.axis_index("tensor")
+    fk, fv = fresh_pair(recv, base, up, gains, cos4, sin4, t)
     row = lax.broadcasted_iota(jnp.int32, (128, 1), 0)
     row_game = lax.rem(row, 16) // 4
     row_step = lax.rem(row, 4)
@@ -166,7 +209,7 @@
     valid = slot < length
     for k in range(KVH):
         q = jnp.concatenate(
-            [recv[4 * k + i, :, HD * j : HD * j + HD] for i in range(4) for j in range(2)], axis=0
+            [recv[4 * k + i, 0:ROWS, HD * j : HD * j + HD] for i in range(4) for j in range(2)], axis=0
         )
         qs[k] = q
         lanes = slice(HD * k, HD * k + HD)
@@ -187,8 +230,8 @@
         accs[k] = acc
     kk, game = t // 4, lax.rem(t, 4)
     zeros = jnp.zeros((120, HD), f32)
-    keys = jnp.concatenate([fk[...], zeros], axis=0).astype(bf16)
-    values = jnp.concatenate([fv[...], zeros], axis=0).astype(bf16)
+    keys = jnp.concatenate([fk, zeros], axis=0).astype(bf16)
+    values = jnp.concatenate([fv, zeros], axis=0).astype(bf16)
     fresh = dot(qs[kk], keys, ((1,), (1,))) * score_scale
     later = lax.broadcasted_iota(jnp.int32, (128, 128), 1)
     causal = jnp.logical_and(row_game == game, later <= row_step)
@@ -305,64 +348,93 @@
 ):
     shape = jax.ShapeDtypeStruct
     cos, sin = rope_tables(lengths)
-    factors = run(
-        pack_factors,
-        shape((N, 24, WIDE), f32),
+    dma = pltpu.SemaphoreType.DMA
+    shared, x, own_x, own_states = run(
+        prepare,
+        (
+            shape((N, 8, WIDE), f32),
+            shape((ROWS, D), bf16),
+            shape((ROWS, COLS), f32),
+            shape((ROWS, COLS), f32),
+        ),
         (
             query_down.T,
-            query_up,
-            pair_down.transpose(0, 2, 1),
             pair_up,
-            output_down.T,
-            output_up,
+            states,
+            key_value_weight,
+            input_gain.astype(f32)[None, :],
         ),
-        "pack_factors",
+        "prepare",
+        specs=[HBM] * 4 + [VMEM],
+        scratch=[
+            pltpu.VMEM((4, COLS), f32),
+            pltpu.VMEM((2, 4, 32), f32),
+            pltpu.VMEM((GAMES, STEPS, D), bf16),
+            pltpu.VMEM((2, COLS, 512), bf16),
+            pltpu.VMEM((ROWS, D), f32),
+            pltpu.VMEM((ROWS, 1024), f32),
+            dma((4,)),
+        ],
+    )
+    shared = exchange(shared, "tensor")
+    factors, base = run(
+        regroup,
+        (shape((N, 72, WIDE), f32), shape((8, WIDE), f32)),
+        (shared, query_up, pair_down.transpose(0, 2, 1), output_down.T, output_up),
+        "regroup",
+        specs=[VMEM] + [HBM] * 4,
+        scratch=[
+            pltpu.VMEM((4, 256), f32),
+            pltpu.VMEM((2, 4, COLS), f32),
+            pltpu.VMEM((4, 256), f32),
+            pltpu.VMEM((4, COLS), f32),
+            dma((4,)),
+        ],
     )
     factors = exchange(factors, "group")
-    shared, x, own_states, up_query, down_output, up_output = run(
-        normalise_input,
+    queries, down_output, up_output, up_pair = run(
+        merge_queries,
         (
-            shape((N, RANK + 8, WIDE), f32),
-            shape((ROWS, D), bf16),
-            shape((ROWS, COLS), f32),
-            shape((RANK, 256), f32),
+            shape((N, 24, 256), bf16),
             shape((RANK, 256), f32),
             shape((RANK, COLS), f32),
+            shape((2, RANK, HD), f32),
         ),
-        (factors, states, input_gain.astype(f32)[None, :], key_value_weight),
-        "normalise_input",
-        scratch=[
-            pltpu.VMEM((ROWS, D), f32),
-            pltpu.VMEM((ROWS, D), f32),
-            pltpu.VMEM((6, RANK, WIDE), f32),
-            pltpu.VMEM((ROWS, 1152), f32),
-        ],
-    )
-    shared = exchange(shared, "tensor")
-    pad = jnp.zeros((GAMES, 4, HD), f32)
-    queries, fresh_keys, fresh_values = run(
-        merge_queries,
-        (shape((N, ROWS, 256), bf16), shape((8, HD), f32), shape((8, HD), f32)),
         (
-            shared,
+            factors,
             query_weight,
             x,
-            up_query,
+            own_x,
             norm_gains,
             cos.reshape(ROWS, HD),
             sin.reshape(ROWS, HD),
+        ),
+        "merge_queries",
+        specs=[VMEM, HBM] + [VMEM] * 5,
+        scratch=[
+            pltpu.VMEM((18, RANK, WIDE), f32),
+            pltpu.VMEM((D, 256), bf16),
+            dma((N // 2,)),
+        ],
+    )
+    queries = exchange(queries, "tensor")
+    pad = jnp.zeros((GAMES, 4, HD), f32)
+    partials = run(
+        attend,
+        shape((N, 40, HD), f32),
+        (
+            lengths,
+            queries,
+            cache_keys,
+            cache_values,
+            base,
+            up_pair,
+            norm_gains,
             jnp.concatenate([cos, pad], axis=1),
             jnp.concatenate([sin, pad], axis=1),
         ),
-        "merge_queries",
-    )
-    queries = exchange(queries, "tensor")
-    partials = run(
-        attend,
-        shape((N, 40, HD), f32),
-        (lengths, queries, cache_keys, cache_values, fresh_keys, fresh_values),
         "attend",
-        specs=[SMEM] + [VMEM] * 5,
+        specs=[SMEM] + [VMEM] * 8,
         scratch=[
             pltpu.VMEM((KVH, 128, HD), bf16),
             pltpu.VMEM((KVH, 128, 1), f32),

time: 153 us -> 141 us (0.922)
  waiting for transfers between devices: 62.9 us -> 43.4 us
  blocking collectives: 43.5 us -> 50.2 us
  starting transfers between devices: 21 us -> 16.2 us
  local copies, waits for them, and re-layouts: 8 us -> 10.4 us
  Pallas kernels: 14.1 us -> 16.3 us
    all_to_all x3, waiting for transfers between devices: 62.9 us -> 43.4 us  [exchange(): return lax.all_to_all(array, axis, 0, 0, tiled=True)]
    all_to_all x3, blocking collectives: 43.5 us -> 50.2 us  [exchange(): return lax.all_to_all(array, axis, 0, 0, tiled=True)]
    all_to_all x3, starting transfers between devices: 21 us -> 16.2 us  [exchange(): return lax.all_to_all(array, axis, 0, 0, tiled=True)]
    unnamed x30, local copies, waits for them, and re-layouts: 7.91 us -> 10.4 us
    pallas_call x7, Pallas kernels: 14.1 us -> 16.3 us  [run(): pl.pallas_call(body, out_shape=outs, in_specs=specs or [VMEM] * len(args)...]
  transfers between devices with their start and end apart: 3 -> 3, of which waited for: 3 -> 3; matrix products, arithmetic and copies ran while one was open for 1% -> 0% of each run, Pallas kernels for 0% -> 0%
where the time goes in v2:
time: 141 us; the launch traced here: 139 us
  blocking collectives  50.2 us (36%)
  waiting for transfers between devices  43.4 us (31%)
  Pallas kernels  16.3 us (12%)
  starting transfers between devices  16.2 us (11%)
  local copies, waits for them, and re-layouts  10.4 us (7%)
    all_to_all x3, blocking collectives, exchange(): return lax.all_to_all(array, axis, 0, 0, tiled=True)  50.2 us
    all_to_all x3, waiting for transfers between devices, exchange(): return lax.all_to_all(array, axis, 0, 0, tiled=True)  43.4 us
    pallas_call x7, Pallas kernels, run(): pl.pallas_call(body, out_shape=outs, in_specs=specs or [VMEM] * len(args)...  16.3 us
    all_to_all x3, starting transfers between devices, exchange(): return lax.all_to_all(array, axis, 0, 0, tiled=True)  16.2 us
    unnamed x30, local copies, waits for them, and re-layouts  10.4 us
  transfers between devices with their start and end apart: 3, of which 3 were waited for; matrix products, arithmetic and copies ran while one was open for 0% of the time, Pallas kernels for 0%

profile of v2, /device:TPU:8, one launch (start us, length us, event | category | flops | bytes accessed | tf_op | source)
XLA Modules:
  0.0 138.6 jit_solution(1272515954630835750)
XLA Ops:
  0.7 0.7 broadcast_in_dim.19
  1.4 1.1 copy-done.4
  2.5 0.9 copy-done.5
  3.4 0.7 copy-done.7
  4.1 0.7 copy-done.9
  4.8 1.2 prepare.1
  5.9 19.5 %all_to_all.30.recv = f32[16,8,384]{2,1,0:T(8,128)S(1)} all-to-all(f32[16,8,384]{2,1,0:T(8,128)S(1)} %get-tuple-element.12), channel_id=1, replica_groups=mesh['group'=16,'tensor'=16] {'tensor'}, dimensions={0} | all-to-all | bytes 393216 | tf_op jit(solution)/shard_map/all_to_all | solution.py:320
  25.4 0.7 copy-done.6
  26.1 0.7 copy-done.8
  26.8 0.7 copy-done.10
  27.5 0.7 copy-done.11
  28.2 1.4 %regroup.1 = (f32[16,72,384]{2,1,0:T(8,128)}, f32[8,384]{1,0:T(8,128)S(1)}) custom-call(f32[16,8,384]{2,1,0:T(8,128)S(1)} %all_to_all.30.recv, f32[4,256]{1,0:T(4,128)S(1)} %copy-done.10, f32[2,4,320]{2,1,0:T(4,128)S(1)} %bitcast.7, f32[4,256]{1,0:T(4,128)S(1)} %bitcast.9, f32[4,320]{1,0:T(4,128)S(1)} %copy-done.8), custom_call_target="tpu_custom_call" | custom-call | tf_op jit(solution)/shard_map/regroup/pallas_call | solution.py:44
  29.7 6.1 %all-to-all-start.1 = ((f32[16,72,384]{2,1,0:T(8,128)}), f32[16,72,384]{2,1,0:T(8,128)S(1)}, u32[]{:S(2)}, u32[]{:S(2)}) async-start(f32[16,72,384]{2,1,0:T(8,128)} %get-tuple-element.13), calls=%async_computation.1 | async-start | bytes 3538944 | tf_op jit(solution)/shard_map/all_to_all | solution.py:320
  35.9 0.1 convert_element_type.14
  36.0 0.1 fusion
  36.2 25.3 %all-to-all-done.1.recv = f32[16,72,384]{2,1,0:T(8,128)S(1)} async-done(((f32[16,72,384]{2,1,0:T(8,128)}), f32[16,72,384]{2,1,0:T(8,128)S(1)}, u32[]{:S(2)}, u32[]{:S(2)}) %all-to-all-start.1) | async-done | bytes 1769504 | tf_op jit(solution)/shard_map/all_to_all | solution.py:320
  61.5 1.7 %copy-done = bf16[5120,256]{1,0:T(8,128)(2,1)S(1)} copy-done((bf16[5120,256]{1,0:T(8,128)(2,1)S(1)}, bf16[5120,256]{1,0:T(8,128)(2,1)}, u32[]{:S(2)}) %copy-start) | copy-done | bytes 2621464
  63.3 8.0 %merge_queries.1 = (bf16[16,24,256]{2,1,0:T(8,128)(2,1)}, f32[64,256]{1,0:T(8,128)S(1)}, f32[64,320]{1,0:T(8,128)S(1)}, f32[2,64,128]{2,1,0:T(8,128)S(1)}) custom-call(f32[16,72,384]{2,1,0:T(8,128)S(1)} %all-to-all-done.1.recv, bf16[5120,256]{1,0:T(8,128)(2,1)S(1)} %copy-done, bf16[16,5120]{1,0:T(8,128)(2,1)S(1)} %get-tuple-element.14.x, ...), custom_call_target="tpu_custom_call" | custom-call | tf_op jit(solution)/shard_map/merge_queries/pallas_call | solution.py:44
  71.3 5.3 %all-to-all-start.2 = ((bf16[16,24,256]{2,1,0:T(8,128)(2,1)}), bf16[16,24,256]{2,1,0:T(8,128)(2,1)S(1)}, u32[]{:S(2)}, u32[]{:S(2)}) async-start(bf16[16,24,256]{2,1,0:T(8,128)(2,1)} %get-tuple-element.16), calls=%async_computation.2 | async-start | bytes 393216 | tf_op jit(solution)/shard_map/all_to_all | solution.py:320
  76.6 0.1 fusion.1
  76.7 0.1 select_maximum_fusion
  76.8 9.3 %all-to-all-done.2.recv = bf16[16,24,256]{2,1,0:T(8,128)(2,1)S(1)} async-done(((bf16[16,24,256]{2,1,0:T(8,128)(2,1)}), bf16[16,24,256]{2,1,0:T(8,128)(2,1)S(1)}, u32[]{:S(2)}, u32[]{:S(2)}) %all-to-all-start.2) | async-done | bytes 196640 | tf_op jit(solution)/shard_map/all_to_all | solution.py:320
  86.1 1.2 copy-done.2
  87.4 1.2 copy-done.3
  88.6 2.9 %attend.1 = f32[16,40,128]{2,1,0:T(8,128)S(1)} custom-call(s32[4]{0:T(128)S(1)} %copy-done.13, bf16[16,24,256]{2,1,0:T(8,128)(2,1)S(1)} %all-to-all-done.2.recv, bf16[4,256,512]{2,1,0:T(8,128)(2,1)S(1)} %copy-done.2, bf16[4,256,512]{2,1,0:T(8,128)(2,1)S(1)} %copy-done.3, f32[8,384]{1,0:T(8,128)S(1)} %get-tuple-element.17.base, ...), custom_call_target="tpu_custom_call" | custom-call | tf_op jit(solution)/shard_map/attend/pallas_call | solution.py:44
  91.5 15.1 %all_to_all.31.recv = f32[16,40,128]{2,1,0:T(8,128)S(1)} all-to-all(f32[16,40,128]{2,1,0:T(8,128)S(1)} %attend.1), channel_id=1, replica_groups=mesh['group'=16,'tensor'=16] {'tensor'}, dimensions={0} | all-to-all | bytes 655360 | tf_op jit(solution)/shard_map/all_to_all | solution.py:320
  106.6 0.8 project.1
  107.4 15.6 %all_to_all.32.recv = f32[16,16,384]{2,1,0:T(8,128)S(1)} all-to-all(f32[16,16,384]{2,1,0:T(8,128)S(1)} %project.1), channel_id=1, replica_groups=mesh['group'=16,'tensor'=16] {'tensor'}, dimensions={0} | all-to-all | bytes 786432 | tf_op jit(solution)/shard_map/all_to_all | solution.py:320
  123.0 1.1 add_residual.1
  124.1 4.8 %all-to-all-start.5 = ((bf16[16,16,384]{2,1,0:T(8,128)(2,1)}), bf16[16,16,384]{2,1,0:T(8,128)(2,1)S(1)}, u32[]{:S(2)}, u32[]{:S(2)}) async-start(bf16[16,16,384]{2,1,0:T(8,128)(2,1)} %add_residual.1), calls=%async_computation.5 | async-start | bytes 393216 | tf_op jit(solution)/shard_map/all_to_all | solution.py:320
  128.9 8.7 %all-to-all-done.5.recv = bf16[16,16,384]{2,1,0:T(8,128)(2,1)S(1)} async-done(((bf16[16,16,384]{2,1,0:T(8,128)(2,1)}), bf16[16,16,384]{2,1,0:T(8,128)(2,1)S(1)}, u32[]{:S(2)}, u32[]{:S(2)}) %all-to-all-start.5) | async-done | bytes 196640 | tf_op jit(solution)/shard_map/all_to_all | solution.py:320
  137.6 0.9 finish.1
  (23 shorter events, 0.2 us)
Async XLA Ops:
  0.6 35.2 %copy-start.13 = (s32[4]{0:T(128)S(1)}, s32[4]{0:T(128)}, u32[]{:S(2)}) copy-start(s32[4]{0:T(128)} %lengths.1) | copy-start | bytes 52
  0.6 60.9 %copy-start.12 = (f32[2,128]{1,0:T(2,128)S(1)}, f32[2,128]{1,0:T(2,128)}, u32[]{:S(2)}) copy-start(f32[2,128]{1,0:T(2,128)} %gains.3) | copy-start | bytes 3076
  1.4 1.1 copy-start.4
  2.5 0.9 copy-start.5
  3.4 0.7 copy-start.7
  4.1 0.7 copy-start.9
  25.4 0.7 copy-start.6
  26.1 0.7 copy-start.8
  26.8 0.7 copy-start.10
  27.5 0.7 copy-start.11
  29.7 31.9 %all-to-all-start.1 = ((f32[16,72,384]{2,1,0:T(8,128)}), f32[16,72,384]{2,1,0:T(8,128)S(1)}, u32[]{:S(2)}, u32[]{:S(2)}) async-start(f32[16,72,384]{2,1,0:T(8,128)} %get-tuple-element.13), calls=%async_computation.1 | async-start | bytes 3538944 | tf_op jit(solution)/shard_map/all_to_all | solution.py:320
  61.5 1.7 %copy-start = (bf16[5120,256]{1,0:T(8,128)(2,1)S(1)}, bf16[5120,256]{1,0:T(8,128)(2,1)}, u32[]{:S(2)}) copy-start(bf16[5120,256]{1,0:T(8,128)(2,1)} %qw_hbm.1) | copy-start | bytes 7864324
  71.3 35.3 %copy-start.1 = (bf16[256,5120]{1,0:T(8,128)(2,1)S(1)}, bf16[256,5120]{1,0:T(8,128)(2,1)}, u32[]{:S(2)}) copy-start(bf16[256,5120]{1,0:T(8,128)(2,1)} %ow.1) | copy-start | bytes 7864324
  71.3 14.8 %all-to-all-start.2 = ((bf16[16,24,256]{2,1,0:T(8,128)(2,1)}), bf16[16,24,256]{2,1,0:T(8,128)(2,1)S(1)}, u32[]{:S(2)}, u32[]{:S(2)}) async-start(bf16[16,24,256]{2,1,0:T(8,128)(2,1)} %get-tuple-element.16), calls=%async_computation.2 | async-start | bytes 393216 | tf_op jit(solution)/shard_map/all_to_all | solution.py:320
  86.1 1.2 copy-start.2
  87.4 1.2 copy-start.3
  106.6 22.3 %copy-start.14 = (bf16[5120]{0:T(1024)(128)(2,1)S(1)}, bf16[5120]{0:T(1024)(128)(2,1)}, u32[]{:S(2)}) copy-start(bf16[5120]{0:T(1024)(128)(2,1)} %param.18) | copy-start | bytes 30724
  124.1 13.5 %all-to-all-start.5 = ((bf16[16,16,384]{2,1,0:T(8,128)(2,1)}), bf16[16,16,384]{2,1,0:T(8,128)(2,1)S(1)}, u32[]{:S(2)}, u32[]{:S(2)}) async-start(bf16[16,16,384]{2,1,0:T(8,128)(2,1)} %add_residual.1), calls=%async_computation.5 | async-start | bytes 393216 | tf_op jit(solution)/shard_map/all_to_all | solution.py:320

commit v3 on v2

--- a/solution.py
+++ b/solution.py
@@ -20,6 +20,8 @@
 COLS = D // N
 WIDE = COLS + RANK
 BLOCK = 256
+FULL = D + 1792
+HALF = FULL // 2
 
 epsilon = 1e-06
 rope_theta = 1000000.0
@@ -40,14 +42,14 @@
     )
 
 
-def run(body, outs, args, name, specs=None, scratch=(), flops=0):
+def run(body, outs, args, name, specs=None, scratch=(), limit=48 << 20):
     return pl.pallas_call(
         body,
         out_shape=outs,
         in_specs=specs or [VMEM] * len(args),
         out_specs=jax.tree.map(lambda _: VMEM, outs),
         scratch_shapes=list(scratch),
-        compiler_params=pltpu.CompilerParams(vmem_limit_bytes=48 << 20),
+        compiler_params=pltpu.CompilerParams(vmem_limit_bytes=limit),
         name=name,
     )(*args)
 
@@ -67,11 +69,18 @@
 
 
 def prepare(
-    qd_hbm, pu_hbm, states_hbm, kvw_hbm, gain, out, x_out, xt_out, st_out,
-    qd, pu, states, kvw, act, part, sems,
+    qd_hbm, pu_hbm, states_hbm, kvw_hbm, gain_hbm, out, x_out, xt_out, st_out,
+    qd, pu, states, kvw, gain, act, part, sems,
 ):
     waits = copies(
-        [(states_hbm, states), (kvw_hbm, kvw), (qd_hbm, qd), (pu_hbm, pu)], sems
+        [
+            (states_hbm, states),
+            (gain_hbm, gain),
+            (kvw_hbm, kvw),
+            (qd_hbm, qd),
+            (pu_hbm, pu),
+        ],
+        sems,
     )
     t = lax.axis_index("tensor")
     waits[0].wait()
@@ -80,16 +89,20 @@
     st_out[...] = own_columns(act, t)
     values = act[...]
     scale = lax.rsqrt(jnp.mean(values * values, axis=-1, keepdims=True) + epsilon)
-    x = (values * scale * gain[...]).astype(bf16)
-    x_out[...] = x
-    act[...] = x.astype(f32)
+    waits[1].wait()
+    gains = gain[...].astype(f32)
+    for c in range(D // 128):
+        lanes = slice(128 * c, 128 * c + 128)
+        x = (values[:, lanes] * scale * gains[c : c + 1, :]).astype(bf16)
+        x_out[:, lanes] = x
+        act[:, lanes] = x.astype(f32)
     xt = own_columns(act, t)
     xt_out[...] = xt
-    waits[1].wait()
+    waits[2].wait()
     for n in range(2):
         part[:, 512 * n : 512 * n + 512] = dot(xt.astype(bf16), kvw[n])
-    waits[2].wait()
-    waits[3].wait()
+    for copy in waits[3:]:
+        copy.wait()
     shared = jnp.concatenate([qd[...], pu[0], pu[1]], axis=1)
     for d in range(N):
         k, g = d // 4, d % 4
@@ -100,25 +113,38 @@
         out[d, 4:8, 256:384] = jnp.zeros((4, 128), f32)
 
 
-def regroup(recv, qu_hbm, pd_hbm, od_hbm, ou_hbm, out, base_out, qu, pd, od, ou, sems):
-    waits = copies([(qu_hbm, qu), (pd_hbm, pd), (od_hbm, od), (ou_hbm, ou)], sems)
+def regroup(recv, own, out, base_out, line):
     t = lax.axis_index("tensor")
     base = recv[0]
     for s in range(1, N):
         base += recv[s]
     base_out[...] = base
-    for copy in waits:
-        copy.wait()
-    spare = [qu[:, 64 * c : 64 * c + 64] for c in range(4)]
-    spare += [od[:, 64 * c : 64 * c + 64] for c in range(4)]
-    spare += [ou[:, 64 * c : 64 * c + 64] for c in range(5)]
-    spare += [recv[4 * (t // 4) + c, 0:4, COLS:WIDE] for c in range(4)]
-    spare += [jnp.zeros((4, 64), f32)]
-    wide = [recv[b, 0:4, 0:COLS] for b in range(N)] + [pd[0], pd[1]]
-    blocks = [jnp.concatenate([w, s], axis=1) for w, s in zip(wide, spare)]
-    piece = jnp.concatenate(blocks, axis=0)
+    for p in range(N // 2):
+        line[:, 640 * p : 640 * p + 640] = jnp.concatenate(
+            [recv[2 * p, 0:4, 0:COLS], recv[2 * p + 1, 0:4, 0:COLS]], axis=1
+        )
+    line[:, D : D + 1536] = own[...]
+    pairs = [recv[4 * (t // 4) + c, 0:4, COLS:WIDE] for c in range(4)]
+    line[:, D + 1536 : FULL] = jnp.concatenate(
+        [c[:, 32 * n : 32 * n + 32] for n in range(2) for c in pairs], axis=1
+    )
     for d in range(N):
-        out[d] = piece
+        out[d] = line[:, HALF * (d % 2) : HALF * (d % 2) + HALF]
+
+
+def assemble(recv, out):
+    for c in range(2):
+        for g in range(N):
+            out[c, 4 * g : 4 * g + 4, :] = recv[g]
+
+
+def columns(recv, start, width):
+    if start + width <= HALF:
+        return recv[0, :, start : start + width]
+    if start >= HALF:
+        return recv[1, :, start - HALF : start - HALF + width]
+    left = recv[0, :, start:HALF]
+    return jnp.concatenate([left, recv[1, :, 0 : start + width - HALF]], axis=1)
 
 
 def rotate(values, cosine, sine):
@@ -136,43 +162,30 @@
     return high, middle, (rest - middle.astype(f32)).astype(bf16)
 
 
-def merge_queries(
-    recv, qw_hbm, x, xt, gains, cos, sin, out, od_out, ou_out, up_out, ranks, qw, sems
-):
-    chunks = N // 2
-    waits = copies(
-        [(qw_hbm.at[pl.ds(640 * p, 640)], qw.at[pl.ds(640 * p, 640)]) for p in range(chunks)], sems
-    )
-    for b in range(18):
-        for g in range(N):
-            ranks[b, 4 * g : 4 * g + 4, :] = recv[g, 4 * b : 4 * b + 4, :]
-    spare = [ranks[b, :, COLS:WIDE] for b in range(17)]
-    up = jnp.concatenate(spare[0:4], axis=1)
-    od_out[...] = jnp.concatenate(spare[4:8], axis=1)
-    ou_out[...] = jnp.concatenate(spare[8:13], axis=1)
+def merge_queries(recv, qwt, x, xt, gains, cos, sin, out, od_out, ou_out, up_out):
+    od_out[...] = columns(recv, 6016, 256)
+    ou_out[...] = columns(recv, 6272, COLS)
     for n in range(2):
-        up_out[n] = jnp.concatenate([c[:, 32 * n : 32 * n + 32] for c in spare[13:17]], axis=1)
-    uh, um, ul = split(up)
-    ups = jnp.concatenate([uh, uh, um, um, ul, uh], axis=0)
+        up_out[n] = columns(recv, 6656 + 128 * n, 128)
+    uh, um, ul = [u.astype(f32) for u in split(columns(recv, 5760, 256))]
+    ups = jnp.concatenate([uh, uh, um, um, ul, uh], axis=0).T.astype(bf16)
     raw = jnp.zeros((ROWS, 256), f32)
-    for p in range(chunks):
-        waits[p].wait()
-        merged = []
-        for b in (2 * p, 2 * p + 1):
-            h, m, l = split(ranks[b].T[0:COLS])
-            hm = jnp.concatenate([h, m], axis=1)
-            hl = jnp.concatenate([h, l], axis=1)
-            update = dot(jnp.concatenate([hm, hm, hl], axis=1), ups)
-            weight = qw[COLS * b : COLS * b + COLS, :].astype(f32)
-            merged.append((weight + 2.0 * update).astype(bf16))
-        raw += dot(x[:, 640 * p : 640 * p + 640], jnp.concatenate(merged, axis=0))
+    for p in range(N // 2):
+        lanes = slice(640 * p, 640 * p + 640)
+        h, m, l = split(columns(recv, 640 * p, 640))
+        update = dot(ups, jnp.concatenate([h, m, h, m, h, l], axis=0))
+        merged = (qwt[:, lanes].astype(f32) + 2.0 * update).astype(bf16)
+        raw += dot(x[:, lanes], merged, ((1,), (1,)))
+    cosine = jnp.concatenate([cos[g] for g in range(GAMES)], axis=0)
+    sine = jnp.concatenate([sin[g] for g in range(GAMES)], axis=0)
     heads = []
     for h in range(2):
         v = head_norm(raw[:, HD * h : HD * h + HD], gains[0:1, :])
-        heads.append(rotate(v, cos[...], sin[...]))
+        heads.append(rotate(v, cosine, sine))
     queries = jnp.concatenate(heads, axis=1).astype(bf16).astype(f32)
     low = [
-        dot(xt[...], ranks[16 + n, :, 0:COLS], ((1,), (1,)), HIGHEST) for n in range(2)
+        dot(xt[...], columns(recv, D + COLS * n, COLS), ((1,), (1,)), HIGHEST)
+        for n in range(2)
     ]
     low = [part.astype(f32) for part in split(jnp.concatenate(low, axis=1))]
     top = jnp.concatenate(low[0:2], axis=1)
@@ -192,7 +205,10 @@
     keys = sums[:, 0:128] + 2.0 * dot(low[:, 0:64], up[0], precision=HIGHEST)
     values = sums[:, 128:256] + 2.0 * dot(low[:, 64:128], up[1], precision=HIGHEST)
     game = lax.rem(t, 4)
-    keys = rotate(head_norm(keys, gains[1:2, :]), cos4[game], sin4[game])
+    zeros = jnp.zeros((4, HD), f32)
+    cosine = jnp.concatenate([cos4[game], zeros], axis=0)
+    sine = jnp.concatenate([sin4[game], zeros], axis=0)
+    keys = rotate(head_norm(keys, gains[1:2, :]), cosine, sine)
     return keys, values
 
 
@@ -304,12 +320,14 @@
         squares += recv[s, :, COLS:WIDE].astype(f32)
     mean = jnp.sum(squares, axis=-1, keepdims=True) * (1.0 / D)
     scale = lax.rsqrt(mean + epsilon)
+    gains = gain[...].astype(f32)
     for p in range(N // 2):
         lanes = slice(640 * p, 640 * p + 640)
         both = jnp.concatenate(
             [recv[2 * p, :, 0:COLS].astype(f32), recv[2 * p + 1, :, 0:COLS].astype(f32)], axis=1
         )
-        scaled = both * scale * gain[:, lanes]
+        own = jnp.concatenate([gains[5 * p + c : 5 * p + c + 1, :] for c in range(5)], axis=1)
+        scaled = both * scale * own
         for g in range(GAMES):
             rows = slice(4 * g, 4 * g + 4)
             residual[g, :, lanes] = both[rows].astype(bf16)
@@ -362,36 +380,47 @@
             pair_up,
             states,
             key_value_weight,
-            input_gain.astype(f32)[None, :],
+            input_gain.reshape(D // 128, 128),
         ),
         "prepare",
-        specs=[HBM] * 4 + [VMEM],
+        specs=[HBM] * 5,
+        limit=60 << 20,
         scratch=[
             pltpu.VMEM((4, COLS), f32),
             pltpu.VMEM((2, 4, 32), f32),
             pltpu.VMEM((GAMES, STEPS, D), bf16),
             pltpu.VMEM((2, COLS, 512), bf16),
+            pltpu.VMEM((D // 128, 128), bf16),
             pltpu.VMEM((ROWS, D), f32),
             pltpu.VMEM((ROWS, 1024), f32),
-            dma((4,)),
+            dma((5,)),
         ],
     )
-    shared = exchange(shared, "tensor")
+    own = jnp.concatenate(
+        [
+            pair_down[0].T,
+            pair_down[1].T,
+            query_up,
+            output_down.T,
+            output_up,
+            jnp.zeros((4, 64), f32),
+        ],
+        axis=1,
+    )
+    shared, own, cos, sin, query_turned = lax.optimization_barrier(
+        (exchange(shared, "tensor"), own, cos, sin, query_weight.T)
+    )
     factors, base = run(
         regroup,
-        (shape((N, 72, WIDE), f32), shape((8, WIDE), f32)),
-        (shared, query_up, pair_down.transpose(0, 2, 1), output_down.T, output_up),
+        (shape((N, 4, HALF), f32), shape((8, WIDE), f32)),
+        (shared, own),
         "regroup",
-        specs=[VMEM] + [HBM] * 4,
-        scratch=[
-            pltpu.VMEM((4, 256), f32),
-            pltpu.VMEM((2, 4, COLS), f32),
-            pltpu.VMEM((4, 256), f32),
-            pltpu.VMEM((4, COLS), f32),
-            dma((4,)),
-        ],
+        scratch=[pltpu.VMEM((4, FULL), f32)],
     )
     factors = exchange(factors, "group")
+    factors = run(assemble, shape((2, RANK, HALF), f32), (factors,), "assemble")
+    pairs = [[2 * i, 2 * i + 1] for i in range(N // 2)]
+    factors = lax.all_to_all(factors, "group", 0, 0, tiled=True, axis_index_groups=pairs)
     queries, down_output, up_output, up_pair = run(
         merge_queries,
         (
@@ -400,25 +429,10 @@
             shape((RANK, COLS), f32),
             shape((2, RANK, HD), f32),
         ),
-        (
-            factors,
-            query_weight,
-            x,
-            own_x,
-            norm_gains,
-            cos.reshape(ROWS, HD),
-            sin.reshape(ROWS, HD),
-        ),
+        (factors, query_turned, x, own_x, norm_gains, cos, sin),
         "merge_queries",
-        specs=[VMEM, HBM] + [VMEM] * 5,
-        scratch=[
-            pltpu.VMEM((18, RANK, WIDE), f32),
-            pltpu.VMEM((D, 256), bf16),
-            dma((N // 2,)),
-        ],
     )
     queries = exchange(queries, "tensor")
-    pad = jnp.zeros((GAMES, 4, HD), f32)
     partials = run(
         attend,
         shape((N, 40, HD), f32),
@@ -430,8 +444,8 @@
             base,
             up_pair,
             norm_gains,
-            jnp.concatenate([cos, pad], axis=1),
-            jnp.concatenate([sin, pad], axis=1),
+            cos,
+            sin,
         ),
         "attend",
         specs=[SMEM] + [VMEM] * 8,
@@ -457,7 +471,7 @@
     return run(
         finish,
         (shape((GAMES, STEPS, D), bf16), shape((GAMES, STEPS, D), bf16)),
-        (pieces, post_gain.astype(f32)[None, :]),
+        (pieces, post_gain.reshape(D // 128, 128)),
         "finish",
     )
 

time: 141 us -> 117 us (0.83); the launches traced: 139 us -> 117 us
  waiting for transfers between devices: 43.4 us -> 4.93 us
  blocking collectives: 50.2 us -> 85.8 us
  local copies, waits for them, and re-layouts: 10.4 us -> 3.86 us
  starting transfers between devices: 16.2 us -> 9.95 us
  Pallas kernels: 16.3 us -> 10.5 us
    all_to_all x3 -> x1, waiting for transfers between devices: 43.4 us -> 4.93 us  [exchange(): return lax.all_to_all(array, axis, 0, 0, tiled=True)]
    all_to_all x3 -> x5, blocking collectives: 50.2 us -> 80.6 us  [exchange(): return lax.all_to_all(array, axis, 0, 0, tiled=True)]
    unnamed x30 -> x25, local copies, waits for them, and re-layouts: 10.4 us -> 3.05 us
    all_to_all x3 -> x1, starting transfers between devices: 16.2 us -> 9.95 us  [exchange(): return lax.all_to_all(array, axis, 0, 0, tiled=True)]
    pallas_call x7 -> x8, Pallas kernels: 16.3 us -> 10.5 us  [run(): pl.pallas_call(body, out_shape=outs, in_specs=specs or [VMEM] * len(args)...]
    all_to_all x0 -> x1, blocking collectives: none -> 5.16 us  [local(): lax.all_to_all(factors, 'group', 0, 0, tiled=True, axis_index_groups=pairs)]
  transfers between devices with their start and end apart: 3 -> 1, of which waited for: 3 -> 1; matrix products, arithmetic and copies ran while one was open for 0% -> 4% of each run, Pallas kernels for 0% -> 0%
where the time goes in v3:
time: 117 us
  blocking collectives  85.8 us (73%)
  Pallas kernels  10.5 us (9%)
  starting transfers between devices  9.95 us (9%)
  waiting for transfers between devices  4.93 us (4%)
  local copies, waits for them, and re-layouts  3.86 us (3%)
    all_to_all x5, blocking collectives, exchange(): return lax.all_to_all(array, axis, 0, 0, tiled=True)  80.6 us
    pallas_call x8, Pallas kernels, run(): pl.pallas_call(body, out_shape=outs, in_specs=specs or [VMEM] * len(args)...  10.5 us
    all_to_all x1, starting transfers between devices, exchange(): return lax.all_to_all(array, axis, 0, 0, tiled=True)  9.95 us
    all_to_all x1, blocking collectives, local(): lax.all_to_all(factors, 'group', 0, 0, tiled=True, axis_index_groups=pairs)  5.16 us
    all_to_all x1, waiting for transfers between devices, exchange(): return lax.all_to_all(array, axis, 0, 0, tiled=True)  4.93 us
    unnamed x25, local copies, waits for them, and re-layouts  3.05 us
  transfers between devices with their start and end apart: 1, of which 1 were waited for; matrix products, arithmetic and copies ran while one was open for 4% of the time, Pallas kernels for 0%

profile of v3, /device:TPU:8, one launch (start us, length us, event | category | flops | bytes accessed | tf_op | source)
XLA Modules:
  0.0 116.8 jit_solution(17805390148931893011)
XLA Ops:
  0.6 2.4 %prepare.1 = (f32[16,8,384]{2,1,0:T(8,128)}, bf16[16,5120]{1,0:T(8,128)(2,1)}, f32[16,320]{1,0:T(8,128)}, f32[16,320]{1,0:T(8,128)}) custom-call(f32[4,320]{1,0:T(4,128)} %bitcast.16, f32[2,4,32]{2,1,0:T(4,128)} %pu_hbm.1, bf16[4,4,5120]{2,1,0:T(4,128)(2,1)} %states_hbm.1, bf16[2,320,512]{2,1,0:T(8,128)(2,1)} %kvw_hbm.1, bf16[40,128]{1,0:T(8,128)(2,1)} %bitcast.15), custom_call_target="tpu_custom_call" | custom-call | tf_op jit(solution)/shard_map/prepare/pallas_call | solution.py:46
  3.0 10.0 %all-to-all-start = ((f32[16,8,384]{2,1,0:T(8,128)}), f32[16,8,384]{2,1,0:T(8,128)S(1)}, u32[]{:S(2)}, u32[]{:S(2)}) async-start(f32[16,8,384]{2,1,0:T(8,128)} %get-tuple-element.17), calls=%async_computation | async-start | bytes 393216 | tf_op jit(solution)/shard_map/all_to_all | solution.py:338
  12.9 0.7 add_convert_fusion
  13.7 0.7 slice_bitcast_fusion
  14.4 0.0 copy-start.9
  14.4 0.0 copy-start.10
  14.4 0.0 copy-start.11
  14.4 3.0 %copy.18 = bf16[5120,256]{0,1:T(8,128)(2,1)S(1)} copy(bf16[5120,256]{1,0:T(8,128)(2,1)} %param.20) | data formatting | bytes 5242880 | tf_op args[4]
  17.4 0.0 copy-done.9
  17.5 0.0 copy-done.10
  17.5 0.0 copy-done.11
  17.5 0.1 concatenate.9.own
  17.6 0.1 fusion
  17.7 0.1 pad_maximum_fusion
  17.8 4.9 %all-to-all-done.recv = f32[16,8,384]{2,1,0:T(8,128)S(1)} async-done(((f32[16,8,384]{2,1,0:T(8,128)}), f32[16,8,384]{2,1,0:T(8,128)S(1)}, u32[]{:S(2)}, u32[]{:S(2)}) %all-to-all-start) | async-done | bytes 196640 | tf_op jit(solution)/shard_map/all_to_all | solution.py:338
  22.7 0.1 regroup.1
  22.9 21.9 %all_to_all.35.recv = f32[16,4,3456]{2,1,0:T(4,128)S(1)} all-to-all(f32[16,4,3456]{2,1,0:T(4,128)S(1)} %get-tuple-element.20), channel_id=1, replica_groups=mesh['group'=16,'tensor'=16] {'group'}, dimensions={0} | all-to-all | bytes 1769472 | tf_op jit(solution)/shard_map/all_to_all | solution.py:338
  44.8 0.2 assemble.1
  45.0 5.2 %all_to_all.36.recv = f32[2,64,3456]{2,1,0:T(8,128)S(1)} all-to-all(f32[2,64,3456]{2,1,0:T(8,128)S(1)} %assemble.1), channel_id=1, replica_groups={{0,16},{32,48},{64,80},{96,112},{128,144},{160,176},{192,208},{224,240}..., dimensions={0} | all-to-all | bytes 3538944 | tf_op jit(solution)/shard_map/all_to_all | solution.py:423
  50.2 0.0 copy-done.3
  50.2 0.0 copy-done.4
  50.2 0.0 copy-done.7
  50.2 2.7 %merge_queries.1 = (bf16[16,24,256]{2,1,0:T(8,128)(2,1)S(1)}, f32[64,256]{1,0:T(8,128)S(1)}, f32[64,320]{1,0:T(8,128)S(1)}, f32[2,64,128]{2,1,0:T(8,128)S(1)}) custom-call(f32[2,64,3456]{2,1,0:T(8,128)S(1)} %all_to_all.36.recv, bf16[256,5120]{1,0:T(8,128)(2,1)S(1)} %bitcast.13, bf16[16,5120]{1,0:T(8,128)(2,1)S(1)} %copy-done.3, f32[16,320]{1,0:T(8,128)S(1)} %copy-done.4, ...), custom_call_target="tpu_custom_call" | custom-call | tf_op jit(solution)/shard_map/merge_queries/pallas_call | solution.py:46
  53.0 0.0 copy-start
  53.0 14.4 %all_to_all.37.recv = bf16[16,24,256]{2,1,0:T(8,128)(2,1)S(1)} all-to-all(bf16[16,24,256]{2,1,0:T(8,128)(2,1)S(1)} %get-tuple-element.26), channel_id=1, replica_groups=mesh['group'=16,'tensor'=16] {'tensor'}, dimensions={0} | all-to-all | bytes 393216 | tf_op jit(solution)/shard_map/all_to_all | solution.py:338
  67.4 2.9 %attend.1 = f32[16,40,128]{2,1,0:T(8,128)S(1)} custom-call(s32[4]{0:T(128)S(1)} %copy-done.8, bf16[16,24,256]{2,1,0:T(8,128)(2,1)S(1)} %all_to_all.37.recv, bf16[4,256,512]{2,1,0:T(8,128)(2,1)S(1)} %copy-done.1, bf16[4,256,512]{2,1,0:T(8,128)(2,1)S(1)} %copy-done.2, f32[8,384]{1,0:T(8,128)S(1)} %get-tuple-element.27.base, ...), custom_call_target="tpu_custom_call" | custom-call | tf_op jit(solution)/shard_map/attend/pallas_call | solution.py:46
  70.3 15.7 %all_to_all.38.recv = f32[16,40,128]{2,1,0:T(8,128)S(1)} all-to-all(f32[16,40,128]{2,1,0:T(8,128)S(1)} %attend.1), channel_id=1, replica_groups=mesh['group'=16,'tensor'=16] {'tensor'}, dimensions={0} | all-to-all | bytes 655360 | tf_op jit(solution)/shard_map/all_to_all | solution.py:338
  86.0 0.8 project.1
  86.8 16.0 %all_to_all.39.recv = f32[16,16,384]{2,1,0:T(8,128)S(1)} all-to-all(f32[16,16,384]{2,1,0:T(8,128)S(1)} %project.1), channel_id=1, replica_groups=mesh['group'=16,'tensor'=16] {'tensor'}, dimensions={0} | all-to-all | bytes 786432 | tf_op jit(solution)/shard_map/all_to_all | solution.py:338
  102.8 0.4 add_residual.1
  103.2 12.6 %all_to_all.40.recv = bf16[16,16,384]{2,1,0:T(8,128)(2,1)S(1)} all-to-all(bf16[16,16,384]{2,1,0:T(8,128)(2,1)S(1)} %add_residual.1), channel_id=1, replica_groups=mesh['group'=16,'tensor'=16] {'tensor'}, dimensions={0} | all-to-all | bytes 393216 | tf_op jit(solution)/shard_map/all_to_all | solution.py:338
  115.8 0.9 finish.1
  (16 shorter events, 0.0 us)
Async XLA Ops:
  3.0 19.7 %all-to-all-start = ((f32[16,8,384]{2,1,0:T(8,128)}), f32[16,8,384]{2,1,0:T(8,128)S(1)}, u32[]{:S(2)}, u32[]{:S(2)}) async-start(f32[16,8,384]{2,1,0:T(8,128)} %get-tuple-element.17), calls=%async_computation | async-start | bytes 393216 | tf_op jit(solution)/shard_map/all_to_all | solution.py:338
  14.4 3.1 %copy-start.9 = (f32[4,320]{1,0:T(4,128)S(1)}, f32[4,320]{1,0:T(4,128)}, u32[]{:S(2)}) copy-start(f32[4,320]{1,0:T(4,128)} %param.28) | copy-start | bytes 15364
  14.4 3.1 %copy-start.10 = (f32[4,256]{1,0:T(4,128)S(1)}, f32[4,256]{1,0:T(4,128)}, u32[]{:S(2)}) copy-start(f32[4,256]{1,0:T(4,128)} %param.24) | copy-start | bytes 12292
  14.4 3.0 %copy-start.11 = (f32[256,4]{0,1:T(4,128)S(1)}, f32[256,4]{0,1:T(4,128)}, u32[]{:S(2)}) copy-start(f32[256,4]{0,1:T(4,128)} %param.27) | copy-start | bytes 12292
  44.8 5.4 %copy-start.3 = (bf16[16,5120]{1,0:T(8,128)(2,1)S(1)}, bf16[16,5120]{1,0:T(8,128)(2,1)}, u32[]{:S(2)}) copy-start(bf16[16,5120]{1,0:T(8,128)(2,1)} %get-tuple-element.22.x) | copy-start | bytes 491524
  44.8 5.4 %copy-start.4 = (f32[16,320]{1,0:T(8,128)S(1)}, f32[16,320]{1,0:T(8,128)}, u32[]{:S(2)}) copy-start(f32[16,320]{1,0:T(8,128)} %get-tuple-element.23.xt) | copy-start | bytes 61444
  44.8 5.4 %copy-start.7 = (f32[2,128]{1,0:T(2,128)S(1)}, f32[2,128]{1,0:T(2,128)}, u32[]{:S(2)}) copy-start(f32[2,128]{1,0:T(2,128)} %gains.3) | copy-start | bytes 3076
  50.2 17.2 %copy-start.1 = (bf16[4,256,512]{2,1,0:T(8,128)(2,1)S(1)}, bf16[4,256,512]{2,1,0:T(8,128)(2,1)}, u32[]{:S(2)}) copy-start(bf16[4,256,512]{2,1,0:T(8,128)(2,1)} %ck.1) | copy-start | bytes 3145732
  50.2 17.2 %copy-start.2 = (bf16[4,256,512]{2,1,0:T(8,128)(2,1)S(1)}, bf16[4,256,512]{2,1,0:T(8,128)(2,1)}, u32[]{:S(2)}) copy-start(bf16[4,256,512]{2,1,0:T(8,128)(2,1)} %cv.1) | copy-start | bytes 3145732
  50.2 17.2 %copy-start.8 = (s32[4]{0:T(128)S(1)}, s32[4]{0:T(128)}, u32[]{:S(2)}) copy-start(s32[4]{0:T(128)} %lengths.1) | copy-start | bytes 52
  53.0 33.0 %copy-start = (bf16[256,5120]{1,0:T(8,128)(2,1)S(1)}, bf16[256,5120]{1,0:T(8,128)(2,1)}, u32[]{:S(2)}) copy-start(bf16[256,5120]{1,0:T(8,128)(2,1)} %ow.1) | copy-start | bytes 7864324
  70.3 32.5 %copy-start.5 = (f32[16,320]{1,0:T(8,128)S(1)}, f32[16,320]{1,0:T(8,128)}, u32[]{:S(2)}) copy-start(f32[16,320]{1,0:T(8,128)} %get-tuple-element.31.st) | copy-start | bytes 61444
  86.0 29.9 %copy-start.6 = (bf16[5120]{0:T(1024)(128)(2,1)S(1)}, bf16[5120]{0:T(1024)(128)(2,1)}, u32[]{:S(2)}) copy-start(bf16[5120]{0:T(1024)(128)(2,1)} %param.18) | copy-start | bytes 30724

commit v4 on v3

--- a/solution.py
+++ b/solution.py
@@ -182,24 +182,21 @@
     for h in range(2):
         v = head_norm(raw[:, HD * h : HD * h + HD], gains[0:1, :])
         heads.append(rotate(v, cosine, sine))
-    queries = jnp.concatenate(heads, axis=1).astype(bf16).astype(f32)
-    low = [
-        dot(xt[...], columns(recv, D + COLS * n, COLS), ((1,), (1,)), HIGHEST)
-        for n in range(2)
-    ]
+    low = [dot(xt[...], columns(recv, D + COLS * n, COLS), ((1,), (1,)), HIGHEST) for n in range(2)]
     low = [part.astype(f32) for part in split(jnp.concatenate(low, axis=1))]
-    top = jnp.concatenate(low[0:2], axis=1)
-    bottom = jnp.concatenate([low[2], jnp.zeros((ROWS, 128), f32)], axis=1)
+    rows = [slice(4 * g, 4 * g + 4) for g in range(GAMES)]
+    queries = [heads[j][r] for r in rows for j in range(2)]
     for d in range(N):
-        rows = slice(4 * (d % 4), 4 * (d % 4) + 4)
-        out[d] = jnp.concatenate([queries, top[rows], bottom[rows]], axis=0).astype(bf16)
+        own = rows[d % 4]
+        piece = queries + [part[own] for part in low] + [jnp.zeros((4, HD), f32)]
+        out[d] = jnp.concatenate(piece, axis=0).astype(bf16)
 
 
 def fresh_pair(recv, base, up, gains, cos4, sin4, t):
-    total = recv[0, 16:24, :].astype(f32)
+    total = recv[0, 32:48, :].astype(f32)
     for s in range(1, N):
-        total += recv[s, 16:24, :].astype(f32)
-    low = total[0:4, 0:128] + total[0:4, 128:256] + total[4:8, 0:128]
+        total += recv[s, 32:48, :].astype(f32)
+    low = total[0:4] + total[4:8] + total[8:12]
     low = jnp.concatenate([low, jnp.zeros((4, 128), f32)], axis=0)
     sums = jnp.concatenate([base[4:8, :], jnp.zeros((4, WIDE), f32)], axis=0)
     keys = sums[:, 0:128] + 2.0 * dot(low[:, 0:64], up[0], precision=HIGHEST)
@@ -212,72 +209,71 @@
     return keys, values
 
 
+def softmax(scores, valid):
+    scores = jnp.where(valid, scores * score_scale, masked_score)
+    peak = jnp.max(scores, axis=-1, keepdims=True)
+    weights = jnp.where(valid, jnp.exp(scores - peak), 0.0)
+    return peak, jnp.sum(weights, axis=-1, keepdims=True), weights.astype(bf16)
+
+
+def as_row(column, eye):
+    return jnp.sum(jnp.where(eye, column, 0.0), axis=0, keepdims=True)
+
+
 def attend(lengths, recv, ck, cv, base, up, gains, cos4, sin4, out, qs, ms, ls, accs):
     t = lax.axis_index("tensor")
     fk, fv = fresh_pair(recv, base, up, gains, cos4, sin4, t)
-    row = lax.broadcasted_iota(jnp.int32, (128, 1), 0)
-    row_game = lax.rem(row, 16) // 4
-    row_step = lax.rem(row, 4)
-    length = jnp.zeros((128, 1), jnp.int32)
-    for g in range(GAMES):
-        length = jnp.where(row_game == g, lengths[g], length)
-    slot = t * BLOCK + lax.broadcasted_iota(jnp.int32, (128, BLOCK), 1)
-    valid = slot < length
-    for k in range(KVH):
-        q = jnp.concatenate(
-            [recv[4 * k + i, 0:ROWS, HD * j : HD * j + HD] for i in range(4) for j in range(2)], axis=0
-        )
-        qs[k] = q
-        lanes = slice(HD * k, HD * k + HD)
-        scores = jnp.zeros((128, BLOCK), f32)
-        for g in range(GAMES):
-            own = dot(q, ck[g, :, lanes], ((1,), (1,)))
-            scores = jnp.where(row_game == g, own, scores)
-        scores = jnp.where(valid, scores * score_scale, masked_score)
-        peak = jnp.max(scores, axis=-1, keepdims=True)
-        weights = jnp.where(valid, jnp.exp(scores - peak), 0.0)
-        ms[k] = peak
-        ls[k] = jnp.sum(weights, axis=-1, keepdims=True)
-        rounded = weights.astype(bf16)
-        acc = jnp.zeros((128, HD), f32)
-        for g in range(GAMES):
-            mine = jnp.where(row_game == g, rounded, jnp.zeros_like(rounded))
-            acc += dot(mine, cv[g, :, lanes])
-        accs[k] = acc
-    kk, game = t // 4, lax.rem(t, 4)
+    slot = t * BLOCK + lax.broadcasted_iota(jnp.int32, (1, BLOCK), 1)
+    pairs = [(k, g) for k in range(KVH) for g in range(GAMES)]
+    lanes = [slice(HD * k, HD * k + HD) for k in range(KVH)]
+    wide = [recv[s, 0:32, :].astype(f32) for s in range(N)]
+    scores = []
+    for k, g in pairs:
+        rows = slice(8 * g, 8 * g + 8)
+        q = jnp.concatenate([w[rows] for w in wide[4 * k : 4 * k + 4]], axis=0).astype(bf16)
+        qs[4 * k + g] = q
+        scores.append(dot(q, ck[g, :, lanes[k]], ((1,), (1,))))
+    valid = [jnp.broadcast_to(slot < lengths[g], (32, BLOCK)) for g in range(GAMES)]
+    valid = jnp.concatenate(valid * KVH, axis=0)
+    peak, total, weights = softmax(jnp.concatenate(scores, axis=0), valid)
+    for n, (k, g) in enumerate(pairs):
+        rows = slice(32 * n, 32 * n + 32)
+        ms[n] = peak[rows]
+        ls[n] = total[rows]
+        accs[n] = dot(weights[rows], cv[g, :, lanes[k]])
     zeros = jnp.zeros((120, HD), f32)
     keys = jnp.concatenate([fk, zeros], axis=0).astype(bf16)
     values = jnp.concatenate([fv, zeros], axis=0).astype(bf16)
-    fresh = dot(qs[kk], keys, ((1,), (1,))) * score_scale
-    later = lax.broadcasted_iota(jnp.int32, (128, 128), 1)
-    causal = jnp.logical_and(row_game == game, later <= row_step)
-    fresh = jnp.where(causal, fresh, masked_score)
-    fresh_peak = jnp.max(fresh, axis=-1, keepdims=True)
-    fresh_weights = jnp.where(causal, jnp.exp(fresh - fresh_peak), 0.0)
-    fresh_sum = jnp.sum(fresh_weights, axis=-1, keepdims=True)
-    fresh_acc = dot(fresh_weights.astype(bf16), values)
-    highest = jnp.maximum(ms[kk], fresh_peak)
-    old, new = jnp.exp(ms[kk] - highest), jnp.exp(fresh_peak - highest)
-    ls[kk] = ls[kk] * old + fresh_sum * new
-    accs[kk] = accs[kk] * old + fresh_acc * new
-    ms[kk] = highest
-    eye = lax.broadcasted_iota(jnp.int32, (128, 128), 0) == later
+    step = lax.rem(lax.broadcasted_iota(jnp.int32, (32, HD), 0), 4)
+    causal = lax.broadcasted_iota(jnp.int32, (32, HD), 1) <= step
+    fresh_peak, fresh_sum, fresh_weights = softmax(dot(qs[t], keys, ((1,), (1,))), causal)
+    fresh_acc = dot(fresh_weights, values)
+    highest = jnp.maximum(ms[t], fresh_peak)
+    old, new = jnp.exp(ms[t] - highest), jnp.exp(fresh_peak - highest)
+    ls[t] = ls[t] * old + fresh_sum * new
+    accs[t] = accs[t] * old + fresh_acc * new
+    ms[t] = highest
+    ones = [lax.broadcasted_iota(jnp.int32, (128, 128), n) for n in range(2)]
+    eye = ones[0] == ones[1]
+    order = [(i, g) for i in range(4) for g in range(GAMES)]
     for k in range(KVH):
-        peaks = jnp.sum(jnp.where(eye, ms[k], 0.0), axis=0, keepdims=True)
-        sums = jnp.sum(jnp.where(eye, ls[k], 0.0), axis=0, keepdims=True)
+        stats = []
+        for ref in (ms, ls):
+            column = [ref[4 * k + g, 8 * i : 8 * i + 8, :] for i, g in order]
+            row = as_row(jnp.concatenate(column, axis=0), eye)
+            stats += [part.astype(f32) for part in split(row)]
+        stats = jnp.concatenate(stats + [jnp.zeros((2, 128), f32)], axis=0)
         for i in range(4):
-            d = 4 * k + i
-            out[d, 0:32, :] = accs[k, 32 * i : 32 * i + 32, :]
-            shift = (128 - 32 * i) % 128
-            a = pltpu.roll(peaks, shift, 1) if shift else peaks
-            b = pltpu.roll(sums, shift, 1) if shift else sums
-            out[d, 32:33, :] = a
-            out[d, 33:34, :] = b
-            out[d, 34:40, :] = jnp.zeros((6, 128), f32)
+            mine = [accs[4 * k + g, 8 * i : 8 * i + 8, :] for g in range(GAMES)]
+            own = pltpu.roll(stats, 128 - 32 * i, 1) if i else stats
+            piece = jnp.concatenate(mine + [own, jnp.zeros((8, 128), f32)], axis=0)
+            out[4 * k + i] = piece.astype(bf16)
 
 
 def project(recv, ow, od, out):
-    peaks, sums = recv[:, 32, :], recv[:, 33, :]
+    tails = [recv[s, 32:48, :].astype(f32) for s in range(N)]
+    peaks = jnp.concatenate([p[0:1] + p[1:2] + p[2:3] for p in tails], axis=0)
+    sums = jnp.concatenate([p[3:4] + p[4:5] + p[5:6] for p in tails], axis=0)
     highest = jnp.max(peaks, axis=0, keepdims=True)
     scale = jnp.exp(peaks - highest)
     total = jnp.sum(sums * scale, axis=0, keepdims=True)
@@ -285,20 +281,23 @@
     share = jnp.concatenate([share, jnp.zeros((112, 128), f32)], axis=0).T
     acc = jnp.zeros((32, HD), f32)
     for s in range(N):
-        acc += recv[s, 0:32, :] * share[0:32, s : s + 1]
-    joint = jnp.concatenate([acc[0:16], acc[16:32]], axis=1)
-    attended = joint.astype(bf16)
+        acc += recv[s, 0:32, :].astype(f32) * share[0:32, s : s + 1]
+    halves = [
+        jnp.concatenate([acc[8 * g + 4 * j : 8 * g + 4 * j + 4] for g in range(GAMES)], axis=0)
+        for j in range(2)
+    ]
+    attended = jnp.concatenate(halves, axis=1).astype(bf16)
     low = dot(attended.astype(f32), od[...], ((1,), (1,)), HIGHEST)
     for p in range(N // 2):
         part = dot(attended, ow[:, 640 * p : 640 * p + 640])
-        out[2 * p] = jnp.concatenate([part[:, 0:COLS], low], axis=1)
-        out[2 * p + 1] = jnp.concatenate([part[:, COLS:640], low], axis=1)
+        out[2 * p] = jnp.concatenate([part[:, 0:COLS], low], axis=1).astype(bf16)
+        out[2 * p + 1] = jnp.concatenate([part[:, COLS:640], low], axis=1).astype(bf16)
 
 
 def add_residual(recv, ou, st, out):
-    total = recv[0]
+    total = recv[0].astype(f32)
     for s in range(1, N):
-        total += recv[s]
+        total += recv[s].astype(f32)
     projected = total[:, 0:COLS] + 2.0 * dot(total[:, COLS:WIDE], ou[...], precision=HIGHEST)
     stream = st[...] + projected
     squares = jnp.sum(stream * stream, axis=-1, keepdims=True)
@@ -424,7 +423,7 @@
     queries, down_output, up_output, up_pair = run(
         merge_queries,
         (
-            shape((N, 24, 256), bf16),
+            shape((N, 48, HD), bf16),
             shape((RANK, 256), f32),
             shape((RANK, COLS), f32),
             shape((2, RANK, HD), f32),
@@ -435,7 +434,7 @@
     queries = exchange(queries, "tensor")
     partials = run(
         attend,
-        shape((N, 40, HD), f32),
+        shape((N, 48, HD), bf16),
         (
             lengths,
             queries,
@@ -450,15 +449,15 @@
         "attend",
         specs=[SMEM] + [VMEM] * 8,
         scratch=[
-            pltpu.VMEM((KVH, 128, HD), bf16),
-            pltpu.VMEM((KVH, 128, 1), f32),
-            pltpu.VMEM((KVH, 128, 1), f32),
-            pltpu.VMEM((KVH, 128, HD), f32),
+            pltpu.VMEM((N, 32, HD), bf16),
+            pltpu.VMEM((N, 32, 1), f32),
+            pltpu.VMEM((N, 32, 1), f32),
+            pltpu.VMEM((N, 32, HD), f32),
         ],
     )
     partials = exchange(partials, "tensor")
     projected = run(
-        project, shape((N, ROWS, WIDE), f32), (partials, output_weight, down_output), "project"
+        project, shape((N, ROWS, WIDE), bf16), (partials, output_weight, down_output), "project"
     )
     projected = exchange(projected, "tensor")
     pieces = run(

time: 117 us -> 111 us (0.949)
  blocking collectives: 85.8 us -> 80.8 us
    all_to_all x5, blocking collectives: 80.6 us -> 75.7 us  [exchange(): return lax.all_to_all(array, axis, 0, 0, tiled=True)]
where the time goes in v4:
time: 111 us
  blocking collectives  80.8 us (73%)
  starting transfers between devices  9.95 us (9%)
  Pallas kernels  9.45 us (9%)
  waiting for transfers between devices  4.93 us (4%)
  local copies, waits for them, and re-layouts  3.86 us (3%)
    all_to_all x5, blocking collectives, exchange(): return lax.all_to_all(array, axis, 0, 0, tiled=True)  75.7 us
    all_to_all x1, starting transfers between devices, exchange(): return lax.all_to_all(array, axis, 0, 0, tiled=True)  9.95 us
    pallas_call x8, Pallas kernels, run(): pl.pallas_call(body, out_shape=outs, in_specs=specs or [VMEM] * len(args)...  9.45 us
    all_to_all x1, blocking collectives, local(): lax.all_to_all(factors, 'group', 0, 0, tiled=True, axis_index_groups=pairs)  5.16 us
    all_to_all x1, waiting for transfers between devices, exchange(): return lax.all_to_all(array, axis, 0, 0, tiled=True)  4.93 us
    unnamed x25, local copies, waits for them, and re-layouts  3.05 us
  transfers between devices with their start and end apart: 1, of which 1 were waited for; matrix products, arithmetic and copies ran while one was open for 4% of the time, Pallas kernels for 0%

profile of v4, /device:TPU:8, one launch (start us, length us, event | category | flops | bytes accessed | tf_op | source)
XLA Modules:
  0.0 110.8 jit_solution(7941744218183724901)
XLA Ops:
  0.6 2.4 %prepare.1 = (f32[16,8,384]{2,1,0:T(8,128)}, bf16[16,5120]{1,0:T(8,128)(2,1)}, f32[16,320]{1,0:T(8,128)}, f32[16,320]{1,0:T(8,128)}) custom-call(f32[4,320]{1,0:T(4,128)} %bitcast.16, f32[2,4,32]{2,1,0:T(4,128)} %pu_hbm.1, bf16[4,4,5120]{2,1,0:T(4,128)(2,1)} %states_hbm.1, bf16[2,320,512]{2,1,0:T(8,128)(2,1)} %kvw_hbm.1, bf16[40,128]{1,0:T(8,128)(2,1)} %bitcast.15), custom_call_target="tpu_custom_call" | custom-call | tf_op jit(solution)/shard_map/prepare/pallas_call | solution.py:46
  3.0 10.0 %all-to-all-start = ((f32[16,8,384]{2,1,0:T(8,128)}), f32[16,8,384]{2,1,0:T(8,128)S(1)}, u32[]{:S(2)}, u32[]{:S(2)}) async-start(f32[16,8,384]{2,1,0:T(8,128)} %get-tuple-element.17), calls=%async_computation | async-start | bytes 393216 | tf_op jit(solution)/shard_map/all_to_all | solution.py:337
  12.9 0.7 add_convert_fusion
  13.7 0.7 slice_bitcast_fusion
  14.4 0.0 copy-start.9
  14.4 0.0 copy-start.10
  14.4 0.0 copy-start.11
  14.4 3.0 %copy.18 = bf16[5120,256]{0,1:T(8,128)(2,1)S(1)} copy(bf16[5120,256]{1,0:T(8,128)(2,1)} %param.20) | data formatting | bytes 5242880 | tf_op args[4]
  17.4 0.0 copy-done.9
  17.5 0.0 copy-done.10
  17.5 0.1 concatenate.9.own
  17.6 0.1 fusion
  17.7 0.1 pad_maximum_fusion
  17.8 4.9 %all-to-all-done.recv = f32[16,8,384]{2,1,0:T(8,128)S(1)} async-done(((f32[16,8,384]{2,1,0:T(8,128)}), f32[16,8,384]{2,1,0:T(8,128)S(1)}, u32[]{:S(2)}, u32[]{:S(2)}) %all-to-all-start) | async-done | bytes 196640 | tf_op jit(solution)/shard_map/all_to_all | solution.py:337
  22.7 0.1 regroup.1
  22.9 21.9 %all_to_all.35.recv = f32[16,4,3456]{2,1,0:T(4,128)S(1)} all-to-all(f32[16,4,3456]{2,1,0:T(4,128)S(1)} %get-tuple-element.20), channel_id=1, replica_groups=mesh['group'=16,'tensor'=16] {'group'}, dimensions={0} | all-to-all | bytes 1769472 | tf_op jit(solution)/shard_map/all_to_all | solution.py:337
  44.8 0.2 assemble.1
  45.0 5.2 %all_to_all.36.recv = f32[2,64,3456]{2,1,0:T(8,128)S(1)} all-to-all(f32[2,64,3456]{2,1,0:T(8,128)S(1)} %assemble.1), channel_id=1, replica_groups={{0,16},{32,48},{64,80},{96,112},{128,144},{160,176},{192,208},{224,240}..., dimensions={0} | all-to-all | bytes 3538944 | tf_op jit(solution)/shard_map/all_to_all | solution.py:422
  50.2 0.0 copy-done.4
  50.2 0.0 copy-done.7
  50.2 2.7 %merge_queries.1 = (bf16[16,48,128]{2,1,0:T(8,128)(2,1)S(1)}, f32[64,256]{1,0:T(8,128)S(1)}, f32[64,320]{1,0:T(8,128)S(1)}, f32[2,64,128]{2,1,0:T(8,128)S(1)}) custom-call(f32[2,64,3456]{2,1,0:T(8,128)S(1)} %all_to_all.36.recv, bf16[256,5120]{1,0:T(8,128)(2,1)S(1)} %bitcast.13, bf16[16,5120]{1,0:T(8,128)(2,1)S(1)} %copy-done.3, f32[16,320]{1,0:T(8,128)S(1)} %copy-done.4, ...), custom_call_target="tpu_custom_call" | custom-call | tf_op jit(solution)/shard_map/merge_queries/pallas_call | solution.py:46
  53.0 0.0 copy-start
  53.0 14.4 %all_to_all.37.recv = bf16[16,48,128]{2,1,0:T(8,128)(2,1)S(1)} all-to-all(bf16[16,48,128]{2,1,0:T(8,128)(2,1)S(1)} %get-tuple-element.26), channel_id=1, replica_groups=mesh['group'=16,'tensor'=16] {'tensor'}, dimensions={0} | all-to-all | bytes 393216 | tf_op jit(solution)/shard_map/all_to_all | solution.py:337
  67.4 0.0 copy-done.8
  67.4 0.0 copy-start.5
  67.4 1.8 %attend.1 = bf16[16,48,128]{2,1,0:T(8,128)(2,1)S(1)} custom-call(s32[4]{0:T(128)S(1)} %copy-done.8, bf16[16,48,128]{2,1,0:T(8,128)(2,1)S(1)} %all_to_all.37.recv, bf16[4,256,512]{2,1,0:T(8,128)(2,1)S(1)} %copy-done.1, bf16[4,256,512]{2,1,0:T(8,128)(2,1)S(1)} %copy-done.2, f32[8,384]{1,0:T(8,128)S(1)} %get-tuple-element.27.base, ...), custom_call_target="tpu_custom_call" | custom-call | tf_op jit(solution)/shard_map/attend/pallas_call | solution.py:46
  69.2 13.6 %all_to_all.38.recv = bf16[16,48,128]{2,1,0:T(8,128)(2,1)S(1)} all-to-all(bf16[16,48,128]{2,1,0:T(8,128)(2,1)S(1)} %attend.1), channel_id=1, replica_groups=mesh['group'=16,'tensor'=16] {'tensor'}, dimensions={0} | all-to-all | bytes 393216 | tf_op jit(solution)/shard_map/all_to_all | solution.py:337
  82.8 0.9 project.1
  83.7 13.0 %all_to_all.39.recv = bf16[16,16,384]{2,1,0:T(8,128)(2,1)S(1)} all-to-all(bf16[16,16,384]{2,1,0:T(8,128)(2,1)S(1)} %project.1), channel_id=1, replica_groups=mesh['group'=16,'tensor'=16] {'tensor'}, dimensions={0} | all-to-all | bytes 393216 | tf_op jit(solution)/shard_map/all_to_all | solution.py:337
  96.7 0.4 add_residual.1
  97.1 12.7 %all_to_all.40.recv = bf16[16,16,384]{2,1,0:T(8,128)(2,1)S(1)} all-to-all(bf16[16,16,384]{2,1,0:T(8,128)(2,1)S(1)} %add_residual.1), channel_id=1, replica_groups=mesh['group'=16,'tensor'=16] {'tensor'}, dimensions={0} | all-to-all | bytes 393216 | tf_op jit(solution)/shard_map/all_to_all | solution.py:337
  109.8 0.9 finish.1
  (16 shorter events, 0.0 us)
Async XLA Ops:
  3.0 19.7 %all-to-all-start = ((f32[16,8,384]{2,1,0:T(8,128)}), f32[16,8,384]{2,1,0:T(8,128)S(1)}, u32[]{:S(2)}, u32[]{:S(2)}) async-start(f32[16,8,384]{2,1,0:T(8,128)} %get-tuple-element.17), calls=%async_computation | async-start | bytes 393216 | tf_op jit(solution)/shard_map/all_to_all | solution.py:337
  14.4 3.1 %copy-start.9 = (f32[4,320]{1,0:T(4,128)S(1)}, f32[4,320]{1,0:T(4,128)}, u32[]{:S(2)}) copy-start(f32[4,320]{1,0:T(4,128)} %param.28) | copy-start | bytes 15364
  14.4 3.1 %copy-start.10 = (f32[4,256]{1,0:T(4,128)S(1)}, f32[4,256]{1,0:T(4,128)}, u32[]{:S(2)}) copy-start(f32[4,256]{1,0:T(4,128)} %param.24) | copy-start | bytes 12292
  14.4 3.0 %copy-start.11 = (f32[256,4]{0,1:T(4,128)S(1)}, f32[256,4]{0,1:T(4,128)}, u32[]{:S(2)}) copy-start(f32[256,4]{0,1:T(4,128)} %param.27) | copy-start | bytes 12292
  44.8 5.4 %copy-start.3 = (bf16[16,5120]{1,0:T(8,128)(2,1)S(1)}, bf16[16,5120]{1,0:T(8,128)(2,1)}, u32[]{:S(2)}) copy-start(bf16[16,5120]{1,0:T(8,128)(2,1)} %get-tuple-element.22.x) | copy-start | bytes 491524
  44.8 5.4 %copy-start.4 = (f32[16,320]{1,0:T(8,128)S(1)}, f32[16,320]{1,0:T(8,128)}, u32[]{:S(2)}) copy-start(f32[16,320]{1,0:T(8,128)} %get-tuple-element.23.xt) | copy-start | bytes 61444
  44.8 5.4 %copy-start.7 = (f32[2,128]{1,0:T(2,128)S(1)}, f32[2,128]{1,0:T(2,128)}, u32[]{:S(2)}) copy-start(f32[2,128]{1,0:T(2,128)} %gains.3) | copy-start | bytes 3076
  50.2 17.2 %copy-start.1 = (bf16[4,256,512]{2,1,0:T(8,128)(2,1)S(1)}, bf16[4,256,512]{2,1,0:T(8,128)(2,1)}, u32[]{:S(2)}) copy-start(bf16[4,256,512]{2,1,0:T(8,128)(2,1)} %ck.1) | copy-start | bytes 3145732
  50.2 17.2 %copy-start.2 = (bf16[4,256,512]{2,1,0:T(8,128)(2,1)S(1)}, bf16[4,256,512]{2,1,0:T(8,128)(2,1)}, u32[]{:S(2)}) copy-start(bf16[4,256,512]{2,1,0:T(8,128)(2,1)} %cv.1) | copy-start | bytes 3145732
  50.2 17.2 %copy-start.8 = (s32[4]{0:T(128)S(1)}, s32[4]{0:T(128)}, u32[]{:S(2)}) copy-start(s32[4]{0:T(128)} %lengths.1) | copy-start | bytes 52
  53.0 29.8 %copy-start = (bf16[256,5120]{1,0:T(8,128)(2,1)S(1)}, bf16[256,5120]{1,0:T(8,128)(2,1)}, u32[]{:S(2)}) copy-start(bf16[256,5120]{1,0:T(8,128)(2,1)} %ow.1) | copy-start | bytes 7864324
  67.4 29.3 %copy-start.5 = (f32[16,320]{1,0:T(8,128)S(1)}, f32[16,320]{1,0:T(8,128)}, u32[]{:S(2)}) copy-start(f32[16,320]{1,0:T(8,128)} %get-tuple-element.31.st) | copy-start | bytes 61444
  69.2 40.7 %copy-start.6 = (bf16[5120]{0:T(1024)(128)(2,1)S(1)}, bf16[5120]{0:T(1024)(128)(2,1)}, u32[]{:S(2)}) copy-start(bf16[5120]{0:T(1024)(128)(2,1)} %param.18) | copy-start | bytes 30724

commit v5 on v4

--- a/solution.py
+++ b/solution.py
@@ -107,17 +107,16 @@
     for d in range(N):
         k, g = d // 4, d % 4
         rows = slice(4 * g, 4 * g + 4)
-        out[d, 0:4, :] = shared
-        out[d, 4:8, 0:128] = part[rows, 128 * k : 128 * k + 128]
-        out[d, 4:8, 128:256] = part[rows, 512 + 128 * k : 640 + 128 * k]
-        out[d, 4:8, 256:384] = jnp.zeros((4, 128), f32)
+        out[d, :, 0:WIDE] = shared
+        out[d, :, WIDE : WIDE + 128] = part[rows, 128 * k : 128 * k + 128]
+        out[d, :, WIDE + 128 : 640] = part[rows, 512 + 128 * k : 640 + 128 * k]
 
 
 def regroup(recv, own, out, base_out, line):
     t = lax.axis_index("tensor")
-    base = recv[0]
+    base = recv[0, :, WIDE:640]
     for s in range(1, N):
-        base += recv[s]
+        base += recv[s, :, WIDE:640]
     base_out[...] = base
     for p in range(N // 2):
         line[:, 640 * p : 640 * p + 640] = jnp.concatenate(
@@ -183,22 +182,22 @@
         v = head_norm(raw[:, HD * h : HD * h + HD], gains[0:1, :])
         heads.append(rotate(v, cosine, sine))
     low = [dot(xt[...], columns(recv, D + COLS * n, COLS), ((1,), (1,)), HIGHEST) for n in range(2)]
-    low = [part.astype(f32) for part in split(jnp.concatenate(low, axis=1))]
+    low = [part.astype(f32) for part in split(jnp.concatenate(low, axis=1))[0:2]]
     rows = [slice(4 * g, 4 * g + 4) for g in range(GAMES)]
     queries = [heads[j][r] for r in rows for j in range(2)]
     for d in range(N):
         own = rows[d % 4]
-        piece = queries + [part[own] for part in low] + [jnp.zeros((4, HD), f32)]
+        piece = queries + [part[own] for part in low]
         out[d] = jnp.concatenate(piece, axis=0).astype(bf16)
 
 
 def fresh_pair(recv, base, up, gains, cos4, sin4, t):
-    total = recv[0, 32:48, :].astype(f32)
+    total = recv[0, 32:40, :].astype(f32)
     for s in range(1, N):
-        total += recv[s, 32:48, :].astype(f32)
-    low = total[0:4] + total[4:8] + total[8:12]
+        total += recv[s, 32:40, :].astype(f32)
+    low = total[0:4] + total[4:8]
     low = jnp.concatenate([low, jnp.zeros((4, 128), f32)], axis=0)
-    sums = jnp.concatenate([base[4:8, :], jnp.zeros((4, WIDE), f32)], axis=0)
+    sums = jnp.concatenate([base[...], jnp.zeros((4, 256), f32)], axis=0)
     keys = sums[:, 0:128] + 2.0 * dot(low[:, 0:64], up[0], precision=HIGHEST)
     values = sums[:, 128:256] + 2.0 * dot(low[:, 64:128], up[1], precision=HIGHEST)
     game = lax.rem(t, 4)
@@ -266,12 +265,12 @@
         for i in range(4):
             mine = [accs[4 * k + g, 8 * i : 8 * i + 8, :] for g in range(GAMES)]
             own = pltpu.roll(stats, 128 - 32 * i, 1) if i else stats
-            piece = jnp.concatenate(mine + [own, jnp.zeros((8, 128), f32)], axis=0)
+            piece = jnp.concatenate(mine + [own], axis=0)
             out[4 * k + i] = piece.astype(bf16)
 
 
 def project(recv, ow, od, out):
-    tails = [recv[s, 32:48, :].astype(f32) for s in range(N)]
+    tails = [recv[s, 32:40, :].astype(f32) for s in range(N)]
     peaks = jnp.concatenate([p[0:1] + p[1:2] + p[2:3] for p in tails], axis=0)
     sums = jnp.concatenate([p[3:4] + p[4:5] + p[5:6] for p in tails], axis=0)
     highest = jnp.max(peaks, axis=0, keepdims=True)
@@ -300,31 +299,31 @@
         total += recv[s].astype(f32)
     projected = total[:, 0:COLS] + 2.0 * dot(total[:, COLS:WIDE], ou[...], precision=HIGHEST)
     stream = st[...] + projected
-    squares = jnp.sum(stream * stream, axis=-1, keepdims=True)
-    high = squares.astype(bf16).astype(f32)
-    middle = (squares - high).astype(bf16).astype(f32)
-    low = squares - high - middle
-    lane = lax.broadcasted_iota(jnp.int32, (ROWS, RANK), 1)
-    tail = jnp.where(lane == 0, high, 0.0)
-    tail = jnp.where(lane == 1, middle, tail)
-    tail = jnp.where(lane == 2, low, tail)
-    piece = jnp.concatenate([stream, tail], axis=1).astype(bf16)
+    tail = jnp.concatenate([stream[0:8, 256:COLS], stream[8:16, 256:COLS]], axis=1)
+    piece = jnp.concatenate([stream[:, 0:128], stream[:, 128:256], tail], axis=0).astype(bf16)
     for d in range(N):
         out[d] = piece
 
 
-def finish(recv, gain, residual, normed):
-    squares = jnp.zeros((ROWS, RANK), f32)
-    for s in range(N):
-        squares += recv[s, :, COLS:WIDE].astype(f32)
+def finish(recv, gain, residual, normed, stream):
+    squares = jnp.zeros((ROWS, 128), f32)
+    for p in range(N // 2):
+        parts = []
+        for s in (2 * p, 2 * p + 1):
+            whole = recv[s].astype(f32)
+            tail = whole[32:40]
+            parts += [whole[0:16], whole[16:32]]
+            parts.append(jnp.concatenate([tail[:, 0:64], tail[:, 64:128]], axis=0))
+        both = jnp.concatenate(parts, axis=1)
+        stream[:, 640 * p : 640 * p + 640] = both
+        for c in range(5):
+            squares += both[:, 128 * c : 128 * c + 128] ** 2
     mean = jnp.sum(squares, axis=-1, keepdims=True) * (1.0 / D)
     scale = lax.rsqrt(mean + epsilon)
     gains = gain[...].astype(f32)
     for p in range(N // 2):
         lanes = slice(640 * p, 640 * p + 640)
-        both = jnp.concatenate(
-            [recv[2 * p, :, 0:COLS].astype(f32), recv[2 * p + 1, :, 0:COLS].astype(f32)], axis=1
-        )
+        both = stream[:, lanes]
         own = jnp.concatenate([gains[5 * p + c : 5 * p + c + 1, :] for c in range(5)], axis=1)
         scaled = both * scale * own
         for g in range(GAMES):
@@ -369,7 +368,7 @@
     shared, x, own_x, own_states = run(
         prepare,
         (
-            shape((N, 8, WIDE), f32),
+            shape((N, 4, 640), f32),
             shape((ROWS, D), bf16),
             shape((ROWS, COLS), f32),
             shape((ROWS, COLS), f32),
@@ -411,7 +410,7 @@
     )
     factors, base = run(
         regroup,
-        (shape((N, 4, HALF), f32), shape((8, WIDE), f32)),
+        (shape((N, 4, HALF), f32), shape((4, 256), f32)),
         (shared, own),
         "regroup",
         scratch=[pltpu.VMEM((4, FULL), f32)],
@@ -423,7 +422,7 @@
     queries, down_output, up_output, up_pair = run(
         merge_queries,
         (
-            shape((N, 48, HD), bf16),
+            shape((N, 40, HD), bf16),
             shape((RANK, 256), f32),
             shape((RANK, COLS), f32),
             shape((2, RANK, HD), f32),
@@ -434,7 +433,7 @@
     queries = exchange(queries, "tensor")
     partials = run(
         attend,
-        shape((N, 48, HD), bf16),
+        shape((N, 40, HD), bf16),
         (
             lengths,
             queries,
@@ -462,7 +461,7 @@
     projected = exchange(projected, "tensor")
     pieces = run(
         add_residual,
-        shape((N, ROWS, WIDE), bf16),
+        shape((N, 40, HD), bf16),
         (projected, up_output, own_states),
         "add_residual",
     )
@@ -472,6 +471,7 @@
         (shape((GAMES, STEPS, D), bf16), shape((GAMES, STEPS, D), bf16)),
         (pieces, post_gain.reshape(D // 128, 128)),
         "finish",
+        scratch=[pltpu.VMEM((ROWS, D), f32)],
     )
 
 

time: 111 us -> 109 us (0.982)
  blocking collectives: 80.8 us -> 79.6 us
    all_to_all x5, blocking collectives: 75.7 us -> 74.4 us  [exchange(): return lax.all_to_all(array, axis, 0, 0, tiled=True)]
where the time goes in v5:
time: 109 us
  blocking collectives  79.6 us (73%)
  starting transfers between devices  9.95 us (9%)
  Pallas kernels  9.39 us (9%)
  waiting for transfers between devices  4.25 us (4%)
  local copies, waits for them, and re-layouts  3.87 us (4%)
    all_to_all x5, blocking collectives, exchange(): return lax.all_to_all(array, axis, 0, 0, tiled=True)  74.4 us
    all_to_all x1, starting transfers between devices, exchange(): return lax.all_to_all(array, axis, 0, 0, tiled=True)  9.95 us
    pallas_call x8, Pallas kernels, run(): pl.pallas_call(body, out_shape=outs, in_specs=specs or [VMEM] * len(args)...  9.39 us
    all_to_all x1, blocking collectives, local(): lax.all_to_all(factors, 'group', 0, 0, tiled=True, axis_index_groups=pairs)  5.16 us
    all_to_all x1, waiting for transfers between devices, exchange(): return lax.all_to_all(array, axis, 0, 0, tiled=True)  4.25 us
    unnamed x25, local copies, waits for them, and re-layouts  3.07 us
  transfers between devices with their start and end apart: 1, of which 1 were waited for; matrix products, arithmetic and copies ran while one was open for 4% of the time, Pallas kernels for 0%

profile of v5, /device:TPU:8, one launch (start us, length us, event | category | flops | bytes accessed | tf_op | source)
XLA Modules:
  0.0 108.7 jit_solution(11358998212738822666)
XLA Ops:
  0.6 2.3 %prepare.1 = (f32[16,4,640]{2,1,0:T(4,128)}, bf16[16,5120]{1,0:T(8,128)(2,1)}, f32[16,320]{1,0:T(8,128)}, f32[16,320]{1,0:T(8,128)}) custom-call(f32[4,320]{1,0:T(4,128)} %bitcast.16, f32[2,4,32]{2,1,0:T(4,128)} %pu_hbm.1, bf16[4,4,5120]{2,1,0:T(4,128)(2,1)} %states_hbm.1, bf16[2,320,512]{2,1,0:T(8,128)(2,1)} %kvw_hbm.1, bf16[40,128]{1,0:T(8,128)(2,1)} %bitcast.15), custom_call_target="tpu_custom_call" | custom-call | tf_op jit(solution)/shard_map/prepare/pallas_call | solution.py:46
  3.0 10.0 %all-to-all-start = ((f32[16,4,640]{2,1,0:T(4,128)}), f32[16,4,640]{2,1,0:T(4,128)S(1)}, u32[]{:S(2)}, u32[]{:S(2)}) async-start(f32[16,4,640]{2,1,0:T(4,128)} %get-tuple-element.17), calls=%async_computation | async-start | bytes 327680 | tf_op jit(solution)/shard_map/all_to_all | solution.py:336
  12.9 0.7 add_convert_fusion
  13.7 0.7 slice_bitcast_fusion
  14.4 3.0 %copy.18 = bf16[5120,256]{0,1:T(8,128)(2,1)S(1)} copy(bf16[5120,256]{1,0:T(8,128)(2,1)} %param.20) | data formatting | bytes 5242880 | tf_op args[4]
  17.4 0.0 copy-done.9
  17.4 0.0 copy-done.10
  17.5 0.0 copy-done.11
  17.5 0.1 concatenate.9.own
  17.6 0.1 fusion
  17.7 0.1 pad_maximum_fusion
  17.8 4.2 %all-to-all-done.recv = f32[16,4,640]{2,1,0:T(4,128)S(1)} async-done(((f32[16,4,640]{2,1,0:T(4,128)}), f32[16,4,640]{2,1,0:T(4,128)S(1)}, u32[]{:S(2)}, u32[]{:S(2)}) %all-to-all-start) | async-done | bytes 163872 | tf_op jit(solution)/shard_map/all_to_all | solution.py:336
  22.0 0.1 regroup.1
  22.2 21.9 %all_to_all.35.recv = f32[16,4,3456]{2,1,0:T(4,128)S(1)} all-to-all(f32[16,4,3456]{2,1,0:T(4,128)S(1)} %get-tuple-element.20), channel_id=1, replica_groups=mesh['group'=16,'tensor'=16] {'group'}, dimensions={0} | all-to-all | bytes 1769472 | tf_op jit(solution)/shard_map/all_to_all | solution.py:336
  44.1 0.2 assemble.1
  44.3 5.2 %all_to_all.36.recv = f32[2,64,3456]{2,1,0:T(8,128)S(1)} all-to-all(f32[2,64,3456]{2,1,0:T(8,128)S(1)} %assemble.1), channel_id=1, replica_groups={{0,16},{32,48},{64,80},{96,112},{128,144},{160,176},{192,208},{224,240}..., dimensions={0} | all-to-all | bytes 3538944 | tf_op jit(solution)/shard_map/all_to_all | solution.py:421
  49.5 0.0 copy-done.3
  49.5 0.0 copy-done.4
  49.5 0.0 copy-done.7
  49.5 2.7 %merge_queries.1 = (bf16[16,40,128]{2,1,0:T(8,128)(2,1)S(1)}, f32[64,256]{1,0:T(8,128)S(1)}, f32[64,320]{1,0:T(8,128)S(1)}, f32[2,64,128]{2,1,0:T(8,128)S(1)}) custom-call(f32[2,64,3456]{2,1,0:T(8,128)S(1)} %all_to_all.36.recv, bf16[256,5120]{1,0:T(8,128)(2,1)S(1)} %bitcast.13, bf16[16,5120]{1,0:T(8,128)(2,1)S(1)} %copy-done.3, f32[16,320]{1,0:T(8,128)S(1)} %copy-done.4, ...), custom_call_target="tpu_custom_call" | custom-call | tf_op jit(solution)/shard_map/merge_queries/pallas_call | solution.py:46
  52.3 0.0 copy-start
  52.3 13.8 %all_to_all.37.recv = bf16[16,40,128]{2,1,0:T(8,128)(2,1)S(1)} all-to-all(bf16[16,40,128]{2,1,0:T(8,128)(2,1)S(1)} %get-tuple-element.26), channel_id=1, replica_groups=mesh['group'=16,'tensor'=16] {'tensor'}, dimensions={0} | all-to-all | bytes 327680 | tf_op jit(solution)/shard_map/all_to_all | solution.py:336
  66.1 0.0 copy-done.1
  66.1 0.0 copy-done.8
  66.1 1.8 %attend.1 = bf16[16,40,128]{2,1,0:T(8,128)(2,1)S(1)} custom-call(s32[4]{0:T(128)S(1)} %copy-done.8, bf16[16,40,128]{2,1,0:T(8,128)(2,1)S(1)} %all_to_all.37.recv, bf16[4,256,512]{2,1,0:T(8,128)(2,1)S(1)} %copy-done.1, bf16[4,256,512]{2,1,0:T(8,128)(2,1)S(1)} %copy-done.2, f32[4,256]{1,0:T(4,128)S(1)} %get-tuple-element.27.base, ...), custom_call_target="tpu_custom_call" | custom-call | tf_op jit(solution)/shard_map/attend/pallas_call | solution.py:46
  67.9 13.2 %all_to_all.38.recv = bf16[16,40,128]{2,1,0:T(8,128)(2,1)S(1)} all-to-all(bf16[16,40,128]{2,1,0:T(8,128)(2,1)S(1)} %attend.1), channel_id=1, replica_groups=mesh['group'=16,'tensor'=16] {'tensor'}, dimensions={0} | all-to-all | bytes 327680 | tf_op jit(solution)/shard_map/all_to_all | solution.py:336
  81.1 0.9 project.1
  82.0 12.6 %all_to_all.39.recv = bf16[16,16,384]{2,1,0:T(8,128)(2,1)S(1)} all-to-all(bf16[16,16,384]{2,1,0:T(8,128)(2,1)S(1)} %project.1), channel_id=1, replica_groups=mesh['group'=16,'tensor'=16] {'tensor'}, dimensions={0} | all-to-all | bytes 393216 | tf_op jit(solution)/shard_map/all_to_all | solution.py:336
  94.6 0.3 add_residual.1
  94.9 12.8 %all_to_all.40.recv = bf16[16,40,128]{2,1,0:T(8,128)(2,1)S(1)} all-to-all(bf16[16,40,128]{2,1,0:T(8,128)(2,1)S(1)} %add_residual.1), channel_id=1, replica_groups=mesh['group'=16,'tensor'=16] {'tensor'}, dimensions={0} | all-to-all | bytes 327680 | tf_op jit(solution)/shard_map/all_to_all | solution.py:336
  107.8 0.0 copy-done.6
  107.8 1.0 finish.1
  (16 shorter events, 0.0 us)
Async XLA Ops:
  3.0 19.1 %all-to-all-start = ((f32[16,4,640]{2,1,0:T(4,128)}), f32[16,4,640]{2,1,0:T(4,128)S(1)}, u32[]{:S(2)}, u32[]{:S(2)}) async-start(f32[16,4,640]{2,1,0:T(4,128)} %get-tuple-element.17), calls=%async_computation | async-start | bytes 327680 | tf_op jit(solution)/shard_map/all_to_all | solution.py:336
  14.4 3.0 %copy-start.9 = (f32[4,320]{1,0:T(4,128)S(1)}, f32[4,320]{1,0:T(4,128)}, u32[]{:S(2)}) copy-start(f32[4,320]{1,0:T(4,128)} %param.28) | copy-start | bytes 15364
  14.4 3.1 %copy-start.10 = (f32[4,256]{1,0:T(4,128)S(1)}, f32[4,256]{1,0:T(4,128)}, u32[]{:S(2)}) copy-start(f32[4,256]{1,0:T(4,128)} %param.24) | copy-start | bytes 12292
  14.4 3.1 %copy-start.11 = (f32[256,4]{0,1:T(4,128)S(1)}, f32[256,4]{0,1:T(4,128)}, u32[]{:S(2)}) copy-start(f32[256,4]{0,1:T(4,128)} %param.27) | copy-start | bytes 12292
  44.1 5.4 %copy-start.3 = (bf16[16,5120]{1,0:T(8,128)(2,1)S(1)}, bf16[16,5120]{1,0:T(8,128)(2,1)}, u32[]{:S(2)}) copy-start(bf16[16,5120]{1,0:T(8,128)(2,1)} %get-tuple-element.22.x) | copy-start | bytes 491524
  44.1 5.4 %copy-start.4 = (f32[16,320]{1,0:T(8,128)S(1)}, f32[16,320]{1,0:T(8,128)}, u32[]{:S(2)}) copy-start(f32[16,320]{1,0:T(8,128)} %get-tuple-element.23.xt) | copy-start | bytes 61444
  44.1 5.4 %copy-start.7 = (f32[2,128]{1,0:T(2,128)S(1)}, f32[2,128]{1,0:T(2,128)}, u32[]{:S(2)}) copy-start(f32[2,128]{1,0:T(2,128)} %gains.3) | copy-start | bytes 3076
  49.5 16.6 %copy-start.1 = (bf16[4,256,512]{2,1,0:T(8,128)(2,1)S(1)}, bf16[4,256,512]{2,1,0:T(8,128)(2,1)}, u32[]{:S(2)}) copy-start(bf16[4,256,512]{2,1,0:T(8,128)(2,1)} %ck.1) | copy-start | bytes 3145732
  49.5 16.6 %copy-start.2 = (bf16[4,256,512]{2,1,0:T(8,128)(2,1)S(1)}, bf16[4,256,512]{2,1,0:T(8,128)(2,1)}, u32[]{:S(2)}) copy-start(bf16[4,256,512]{2,1,0:T(8,128)(2,1)} %cv.1) | copy-start | bytes 3145732
  49.5 16.6 %copy-start.8 = (s32[4]{0:T(128)S(1)}, s32[4]{0:T(128)}, u32[]{:S(2)}) copy-start(s32[4]{0:T(128)} %lengths.1) | copy-start | bytes 52
  52.3 28.9 %copy-start = (bf16[256,5120]{1,0:T(8,128)(2,1)S(1)}, bf16[256,5120]{1,0:T(8,128)(2,1)}, u32[]{:S(2)}) copy-start(bf16[256,5120]{1,0:T(8,128)(2,1)} %ow.1) | copy-start | bytes 7864324
  66.1 28.5 %copy-start.5 = (f32[16,320]{1,0:T(8,128)S(1)}, f32[16,320]{1,0:T(8,128)}, u32[]{:S(2)}) copy-start(f32[16,320]{1,0:T(8,128)} %get-tuple-element.31.st) | copy-start | bytes 61444
  67.9 39.9 %copy-start.6 = (bf16[5120]{0:T(1024)(128)(2,1)S(1)}, bf16[5120]{0:T(1024)(128)(2,1)}, u32[]{:S(2)}) copy-start(bf16[5120]{0:T(1024)(128)(2,1)} %param.18) | copy-start | bytes 30724

commit v6 on v5

--- a/solution.py
+++ b/solution.py
@@ -18,6 +18,8 @@
 RANK = 64
 D = 5120
 COLS = D // N
+ORDER = list(range(0, N, 2)) + list(range(1, N, 2))
+PLACE = [ORDER.index(t) for t in range(N)]
 WIDE = COLS + RANK
 BLOCK = 256
 FULL = D + 1792
@@ -107,9 +109,9 @@
     for d in range(N):
         k, g = d // 4, d % 4
         rows = slice(4 * g, 4 * g + 4)
-        out[d, :, 0:WIDE] = shared
-        out[d, :, WIDE : WIDE + 128] = part[rows, 128 * k : 128 * k + 128]
-        out[d, :, WIDE + 128 : 640] = part[rows, 512 + 128 * k : 640 + 128 * k]
+        out[PLACE[d], :, 0:WIDE] = shared
+        out[PLACE[d], :, WIDE : WIDE + 128] = part[rows, 128 * k : 128 * k + 128]
+        out[PLACE[d], :, WIDE + 128 : 640] = part[rows, 512 + 128 * k : 640 + 128 * k]
 
 
 def regroup(recv, own, out, base_out, line):
@@ -120,10 +122,10 @@
     base_out[...] = base
     for p in range(N // 2):
         line[:, 640 * p : 640 * p + 640] = jnp.concatenate(
-            [recv[2 * p, 0:4, 0:COLS], recv[2 * p + 1, 0:4, 0:COLS]], axis=1
+            [recv[PLACE[2 * p + c], 0:4, 0:COLS] for c in range(2)], axis=1
         )
     line[:, D : D + 1536] = own[...]
-    pairs = [recv[4 * (t // 4) + c, 0:4, COLS:WIDE] for c in range(4)]
+    pairs = [recv[2 * (t // 4) + PLACE[c], 0:4, COLS:WIDE] for c in range(4)]
     line[:, D + 1536 : FULL] = jnp.concatenate(
         [c[:, 32 * n : 32 * n + 32] for n in range(2) for c in pairs], axis=1
     )
@@ -188,7 +190,7 @@
     for d in range(N):
         own = rows[d % 4]
         piece = queries + [part[own] for part in low]
-        out[d] = jnp.concatenate(piece, axis=0).astype(bf16)
+        out[PLACE[d]] = jnp.concatenate(piece, axis=0).astype(bf16)
 
 
 def fresh_pair(recv, base, up, gains, cos4, sin4, t):
@@ -225,7 +227,7 @@
     slot = t * BLOCK + lax.broadcasted_iota(jnp.int32, (1, BLOCK), 1)
     pairs = [(k, g) for k in range(KVH) for g in range(GAMES)]
     lanes = [slice(HD * k, HD * k + HD) for k in range(KVH)]
-    wide = [recv[s, 0:32, :].astype(f32) for s in range(N)]
+    wide = [recv[PLACE[s], 0:32, :].astype(f32) for s in range(N)]
     scores = []
     for k, g in pairs:
         rows = slice(8 * g, 8 * g + 8)
@@ -266,7 +268,7 @@
             mine = [accs[4 * k + g, 8 * i : 8 * i + 8, :] for g in range(GAMES)]
             own = pltpu.roll(stats, 128 - 32 * i, 1) if i else stats
             piece = jnp.concatenate(mine + [own], axis=0)
-            out[4 * k + i] = piece.astype(bf16)
+            out[PLACE[4 * k + i]] = piece.astype(bf16)
 
 
 def project(recv, ow, od, out):
@@ -289,8 +291,8 @@
     low = dot(attended.astype(f32), od[...], ((1,), (1,)), HIGHEST)
     for p in range(N // 2):
         part = dot(attended, ow[:, 640 * p : 640 * p + 640])
-        out[2 * p] = jnp.concatenate([part[:, 0:COLS], low], axis=1).astype(bf16)
-        out[2 * p + 1] = jnp.concatenate([part[:, COLS:640], low], axis=1).astype(bf16)
+        out[PLACE[2 * p]] = jnp.concatenate([part[:, 0:COLS], low], axis=1).astype(bf16)
+        out[PLACE[2 * p + 1]] = jnp.concatenate([part[:, COLS:640], low], axis=1).astype(bf16)
 
 
 def add_residual(recv, ou, st, out):
@@ -310,7 +312,7 @@
     for p in range(N // 2):
         parts = []
         for s in (2 * p, 2 * p + 1):
-            whole = recv[s].astype(f32)
+            whole = recv[PLACE[s]].astype(f32)
             tail = whole[32:40]
             parts += [whole[0:16], whole[16:32]]
             parts.append(jnp.concatenate([tail[:, 0:64], tail[:, 64:128]], axis=0))
@@ -333,7 +335,8 @@
 
 
 def exchange(array, axis):
-    return lax.all_to_all(array, axis, 0, 0, tiled=True)
+    groups = [ORDER] if axis == "tensor" else None
+    return lax.all_to_all(array, axis, 0, 0, tiled=True, axis_index_groups=groups)
 
 
 def rope_tables(lengths):

time: 109 us -> 106 us (0.972)
  blocking collectives: 79.6 us -> 77 us
    all_to_all x5, blocking collectives: 74.4 us -> 71.8 us  [exchange(): lax.all_to_all(array, axis, 0, 0, tiled=True, axis_index_groups=groups)]
  transfers between devices with their start and end apart: 1 -> 1, of which waited for: 1 -> 1; matrix products, arithmetic and copies ran while one was open for 4% -> 5% of each run, Pallas kernels for 0% -> 0%
where the time goes in v6:
time: 106 us; the launch traced here: 105 us
  blocking collectives  77 us (73%)
  starting transfers between devices  9.95 us (9%)
  Pallas kernels  9.39 us (9%)
  local copies, waits for them, and re-layouts  3.87 us (4%)
  waiting for transfers between devices  3.17 us (3%)
    all_to_all x5, blocking collectives, exchange(): lax.all_to_all(array, axis, 0, 0, tiled=True, axis_index_groups=groups)  71.8 us
    all_to_all x1, starting transfers between devices, exchange(): lax.all_to_all(array, axis, 0, 0, tiled=True, axis_index_groups=groups)  9.95 us
    pallas_call x8, Pallas kernels, run(): pl.pallas_call(body, out_shape=outs, in_specs=specs or [VMEM] * len(args)...  9.39 us
    all_to_all x1, blocking collectives, local(): lax.all_to_all(factors, 'group', 0, 0, tiled=True, axis_index_groups=pairs)  5.16 us
    all_to_all x1, waiting for transfers between devices, exchange(): lax.all_to_all(array, axis, 0, 0, tiled=True, axis_index_groups=groups)  3.17 us
    unnamed x25, local copies, waits for them, and re-layouts  3.07 us
  transfers between devices with their start and end apart: 1, of which 1 were waited for; matrix products, arithmetic and copies ran while one was open for 5% of the time, Pallas kernels for 0%

profile of v6, /device:TPU:8, one launch (start us, length us, event | category | flops | bytes accessed | tf_op | source)
XLA Modules:
  0.0 105.1 jit_solution(14708618319513287807)
XLA Ops:
  0.6 2.3 %prepare.1 = (f32[16,4,640]{2,1,0:T(4,128)}, bf16[16,5120]{1,0:T(8,128)(2,1)}, f32[16,320]{1,0:T(8,128)}, f32[16,320]{1,0:T(8,128)}) custom-call(f32[4,320]{1,0:T(4,128)} %bitcast.16, f32[2,4,32]{2,1,0:T(4,128)} %pu_hbm.1, bf16[4,4,5120]{2,1,0:T(4,128)(2,1)} %states_hbm.1, bf16[2,320,512]{2,1,0:T(8,128)(2,1)} %kvw_hbm.1, bf16[40,128]{1,0:T(8,128)(2,1)} %bitcast.15), custom_call_target="tpu_custom_call" | custom-call | tf_op jit(solution)/shard_map/prepare/pallas_call | solution.py:48
  3.0 10.0 %all-to-all-start = ((f32[16,4,640]{2,1,0:T(4,128)}), f32[16,4,640]{2,1,0:T(4,128)S(1)}, u32[]{:S(2)}, u32[]{:S(2)}) async-start(f32[16,4,640]{2,1,0:T(4,128)} %get-tuple-element.17), calls=%async_computation | async-start | bytes 327680 | tf_op jit(solution)/shard_map/all_to_all | solution.py:339
  13.0 0.7 add_convert_fusion
  13.7 0.7 slice_bitcast_fusion
  14.4 3.0 %copy.18 = bf16[5120,256]{0,1:T(8,128)(2,1)S(1)} copy(bf16[5120,256]{1,0:T(8,128)(2,1)} %param.20) | data formatting | bytes 5242880 | tf_op args[4]
  17.4 0.0 copy-done.9
  17.4 0.0 copy-done.10
  17.5 0.0 copy-done.11
  17.5 0.1 concatenate.9.own
  17.6 0.1 fusion
  17.7 0.1 pad_maximum_fusion
  17.8 3.2 %all-to-all-done.recv = f32[16,4,640]{2,1,0:T(4,128)S(1)} async-done(((f32[16,4,640]{2,1,0:T(4,128)}), f32[16,4,640]{2,1,0:T(4,128)S(1)}, u32[]{:S(2)}, u32[]{:S(2)}) %all-to-all-start) | async-done | bytes 163872 | tf_op jit(solution)/shard_map/all_to_all | solution.py:339
  21.0 0.1 regroup.1
  21.1 21.9 %all_to_all.35.recv = f32[16,4,3456]{2,1,0:T(4,128)S(1)} all-to-all(f32[16,4,3456]{2,1,0:T(4,128)S(1)} %get-tuple-element.20), channel_id=1, replica_groups=mesh['group'=16,'tensor'=16] {'group'}, dimensions={0} | all-to-all | bytes 1769472 | tf_op jit(solution)/shard_map/all_to_all | solution.py:339
  43.0 0.2 assemble.1
  43.3 5.2 %all_to_all.36.recv = f32[2,64,3456]{2,1,0:T(8,128)S(1)} all-to-all(f32[2,64,3456]{2,1,0:T(8,128)S(1)} %assemble.1), channel_id=1, replica_groups={{0,16},{32,48},{64,80},{96,112},{128,144},{160,176},{192,208},{224,240}..., dimensions={0} | all-to-all | bytes 3538944 | tf_op jit(solution)/shard_map/all_to_all | solution.py:424
  48.4 0.0 copy-done.3
  48.4 0.0 copy-done.4
  48.4 0.0 copy-done.7
  48.5 2.7 %merge_queries.1 = (bf16[16,40,128]{2,1,0:T(8,128)(2,1)S(1)}, f32[64,256]{1,0:T(8,128)S(1)}, f32[64,320]{1,0:T(8,128)S(1)}, f32[2,64,128]{2,1,0:T(8,128)S(1)}) custom-call(f32[2,64,3456]{2,1,0:T(8,128)S(1)} %all_to_all.36.recv, bf16[256,5120]{1,0:T(8,128)(2,1)S(1)} %bitcast.13, bf16[16,5120]{1,0:T(8,128)(2,1)S(1)} %copy-done.3, f32[16,320]{1,0:T(8,128)S(1)} %copy-done.4, ...), custom_call_target="tpu_custom_call" | custom-call | tf_op jit(solution)/shard_map/merge_queries/pallas_call | solution.py:48
  51.2 0.0 copy-start
  51.2 13.3 %all_to_all.37.recv = bf16[16,40,128]{2,1,0:T(8,128)(2,1)S(1)} all-to-all(bf16[16,40,128]{2,1,0:T(8,128)(2,1)S(1)} %get-tuple-element.26), channel_id=1, replica_groups={{0,2,4,6,8,10,12,14,1,3,5,7,9,11,13,15},{16,18,20,22,24,26,28,30,17,19,..., dimensions={0} | all-to-all | bytes 327680 | tf_op jit(solution)/shard_map/all_to_all | solution.py:339
  64.5 0.0 copy-done.1
  64.5 0.0 copy-start.5
  64.5 1.8 %attend.1 = bf16[16,40,128]{2,1,0:T(8,128)(2,1)S(1)} custom-call(s32[4]{0:T(128)S(1)} %copy-done.8, bf16[16,40,128]{2,1,0:T(8,128)(2,1)S(1)} %all_to_all.37.recv, bf16[4,256,512]{2,1,0:T(8,128)(2,1)S(1)} %copy-done.1, bf16[4,256,512]{2,1,0:T(8,128)(2,1)S(1)} %copy-done.2, f32[4,256]{1,0:T(4,128)S(1)} %get-tuple-element.27.base, ...), custom_call_target="tpu_custom_call" | custom-call | tf_op jit(solution)/shard_map/attend/pallas_call | solution.py:48
  66.3 12.3 %all_to_all.38.recv = bf16[16,40,128]{2,1,0:T(8,128)(2,1)S(1)} all-to-all(bf16[16,40,128]{2,1,0:T(8,128)(2,1)S(1)} %attend.1), channel_id=1, replica_groups={{0,2,4,6,8,10,12,14,1,3,5,7,9,11,13,15},{16,18,20,22,24,26,28,30,17,19,..., dimensions={0} | all-to-all | bytes 327680 | tf_op jit(solution)/shard_map/all_to_all | solution.py:339
  78.6 0.9 project.1
  79.4 12.3 %all_to_all.39.recv = bf16[16,16,384]{2,1,0:T(8,128)(2,1)S(1)} all-to-all(bf16[16,16,384]{2,1,0:T(8,128)(2,1)S(1)} %project.1), channel_id=1, replica_groups={{0,2,4,6,8,10,12,14,1,3,5,7,9,11,13,15},{16,18,20,22,24,26,28,30,17,19,..., dimensions={0} | all-to-all | bytes 393216 | tf_op jit(solution)/shard_map/all_to_all | solution.py:339
  91.7 0.3 add_residual.1
  92.0 12.1 %all_to_all.40.recv = bf16[16,40,128]{2,1,0:T(8,128)(2,1)S(1)} all-to-all(bf16[16,40,128]{2,1,0:T(8,128)(2,1)S(1)} %add_residual.1), channel_id=1, replica_groups={{0,2,4,6,8,10,12,14,1,3,5,7,9,11,13,15},{16,18,20,22,24,26,28,30,17,19,..., dimensions={0} | all-to-all | bytes 327680 | tf_op jit(solution)/shard_map/all_to_all | solution.py:339
  104.1 0.0 copy-done.6
  104.1 1.0 finish.1
  (16 shorter events, 0.0 us)
Async XLA Ops:
  3.0 18.0 %all-to-all-start = ((f32[16,4,640]{2,1,0:T(4,128)}), f32[16,4,640]{2,1,0:T(4,128)S(1)}, u32[]{:S(2)}, u32[]{:S(2)}) async-start(f32[16,4,640]{2,1,0:T(4,128)} %get-tuple-element.17), calls=%async_computation | async-start | bytes 327680 | tf_op jit(solution)/shard_map/all_to_all | solution.py:339
  14.4 3.0 %copy-start.9 = (f32[4,320]{1,0:T(4,128)S(1)}, f32[4,320]{1,0:T(4,128)}, u32[]{:S(2)}) copy-start(f32[4,320]{1,0:T(4,128)} %param.28) | copy-start | bytes 15364
  14.4 3.1 %copy-start.10 = (f32[4,256]{1,0:T(4,128)S(1)}, f32[4,256]{1,0:T(4,128)}, u32[]{:S(2)}) copy-start(f32[4,256]{1,0:T(4,128)} %param.24) | copy-start | bytes 12292
  14.4 3.1 %copy-start.11 = (f32[256,4]{0,1:T(4,128)S(1)}, f32[256,4]{0,1:T(4,128)}, u32[]{:S(2)}) copy-start(f32[256,4]{0,1:T(4,128)} %param.27) | copy-start | bytes 12292
  43.0 5.4 %copy-start.3 = (bf16[16,5120]{1,0:T(8,128)(2,1)S(1)}, bf16[16,5120]{1,0:T(8,128)(2,1)}, u32[]{:S(2)}) copy-start(bf16[16,5120]{1,0:T(8,128)(2,1)} %get-tuple-element.22.x) | copy-start | bytes 491524
  43.0 5.4 %copy-start.4 = (f32[16,320]{1,0:T(8,128)S(1)}, f32[16,320]{1,0:T(8,128)}, u32[]{:S(2)}) copy-start(f32[16,320]{1,0:T(8,128)} %get-tuple-element.23.xt) | copy-start | bytes 61444
  43.0 5.4 %copy-start.7 = (f32[2,128]{1,0:T(2,128)S(1)}, f32[2,128]{1,0:T(2,128)}, u32[]{:S(2)}) copy-start(f32[2,128]{1,0:T(2,128)} %gains.3) | copy-start | bytes 3076
  48.4 16.1 %copy-start.1 = (bf16[4,256,512]{2,1,0:T(8,128)(2,1)S(1)}, bf16[4,256,512]{2,1,0:T(8,128)(2,1)}, u32[]{:S(2)}) copy-start(bf16[4,256,512]{2,1,0:T(8,128)(2,1)} %ck.1) | copy-start | bytes 3145732
  48.4 16.1 %copy-start.2 = (bf16[4,256,512]{2,1,0:T(8,128)(2,1)S(1)}, bf16[4,256,512]{2,1,0:T(8,128)(2,1)}, u32[]{:S(2)}) copy-start(bf16[4,256,512]{2,1,0:T(8,128)(2,1)} %cv.1) | copy-start | bytes 3145732
  48.4 16.1 %copy-start.8 = (s32[4]{0:T(128)S(1)}, s32[4]{0:T(128)}, u32[]{:S(2)}) copy-start(s32[4]{0:T(128)} %lengths.1) | copy-start | bytes 52
  51.2 27.4 %copy-start = (bf16[256,5120]{1,0:T(8,128)(2,1)S(1)}, bf16[256,5120]{1,0:T(8,128)(2,1)}, u32[]{:S(2)}) copy-start(bf16[256,5120]{1,0:T(8,128)(2,1)} %ow.1) | copy-start | bytes 7864324
  64.5 27.2 %copy-start.5 = (f32[16,320]{1,0:T(8,128)S(1)}, f32[16,320]{1,0:T(8,128)}, u32[]{:S(2)}) copy-start(f32[16,320]{1,0:T(8,128)} %get-tuple-element.31.st) | copy-start | bytes 61444
  66.3 37.8 %copy-start.6 = (bf16[5120]{0:T(1024)(128)(2,1)S(1)}, bf16[5120]{0:T(1024)(128)(2,1)}, u32[]{:S(2)}) copy-start(bf16[5120]{0:T(1024)(128)(2,1)} %param.18) | copy-start | bytes 30724

commit v7 on v6

--- a/solution.py
+++ b/solution.py
@@ -18,7 +18,7 @@
 RANK = 64
 D = 5120
 COLS = D // N
-ORDER = list(range(0, N, 2)) + list(range(1, N, 2))
+ORDER = [t for first in (0, 2, 1, 3) for t in range(first, N, 4)]
 PLACE = [ORDER.index(t) for t in range(N)]
 WIDE = COLS + RANK
 BLOCK = 256
@@ -125,7 +125,7 @@
             [recv[PLACE[2 * p + c], 0:4, 0:COLS] for c in range(2)], axis=1
         )
     line[:, D : D + 1536] = own[...]
-    pairs = [recv[2 * (t // 4) + PLACE[c], 0:4, COLS:WIDE] for c in range(4)]
+    pairs = [recv[t // 4 + PLACE[c], 0:4, COLS:WIDE] for c in range(4)]
     line[:, D + 1536 : FULL] = jnp.concatenate(
         [c[:, 32 * n : 32 * n + 32] for n in range(2) for c in pairs], axis=1
     )

time: 106 us -> 106 us (level)
  no operation moved by 1% of the time
where the time goes in v7:
time: 106 us; the launch traced here: 105 us
  blocking collectives  77.2 us (73%)
  starting transfers between devices  9.95 us (9%)
  Pallas kernels  9.39 us (9%)
  local copies, waits for them, and re-layouts  3.87 us (4%)
  waiting for transfers between devices  3.25 us (3%)
    all_to_all x5, blocking collectives, exchange(): lax.all_to_all(array, axis, 0, 0, tiled=True, axis_index_groups=groups)  72 us
    all_to_all x1, starting transfers between devices, exchange(): lax.all_to_all(array, axis, 0, 0, tiled=True, axis_index_groups=groups)  9.95 us
    pallas_call x8, Pallas kernels, run(): pl.pallas_call(body, out_shape=outs, in_specs=specs or [VMEM] * len(args)...  9.39 us
    all_to_all x1, blocking collectives, local(): lax.all_to_all(factors, 'group', 0, 0, tiled=True, axis_index_groups=pairs)  5.16 us
    all_to_all x1, waiting for transfers between devices, exchange(): lax.all_to_all(array, axis, 0, 0, tiled=True, axis_index_groups=groups)  3.25 us
    unnamed x25, local copies, waits for them, and re-layouts  3.07 us
  transfers between devices with their start and end apart: 1, of which 1 were waited for; matrix products, arithmetic and copies ran while one was open for 5% of the time, Pallas kernels for 0%

profile of v7, /device:TPU:8, one launch (start us, length us, event | category | flops | bytes accessed | tf_op | source)
XLA Modules:
  0.0 105.4 jit_solution(14309704513518267696)
XLA Ops:
  0.6 2.3 %prepare.1 = (f32[16,4,640]{2,1,0:T(4,128)}, bf16[16,5120]{1,0:T(8,128)(2,1)}, f32[16,320]{1,0:T(8,128)}, f32[16,320]{1,0:T(8,128)}) custom-call(f32[4,320]{1,0:T(4,128)} %bitcast.16, f32[2,4,32]{2,1,0:T(4,128)} %pu_hbm.1, bf16[4,4,5120]{2,1,0:T(4,128)(2,1)} %states_hbm.1, bf16[2,320,512]{2,1,0:T(8,128)(2,1)} %kvw_hbm.1, bf16[40,128]{1,0:T(8,128)(2,1)} %bitcast.15), custom_call_target="tpu_custom_call" | custom-call | tf_op jit(solution)/shard_map/prepare/pallas_call | solution.py:48
  3.0 10.0 %all-to-all-start = ((f32[16,4,640]{2,1,0:T(4,128)}), f32[16,4,640]{2,1,0:T(4,128)S(1)}, u32[]{:S(2)}, u32[]{:S(2)}) async-start(f32[16,4,640]{2,1,0:T(4,128)} %get-tuple-element.17), calls=%async_computation | async-start | bytes 327680 | tf_op jit(solution)/shard_map/all_to_all | solution.py:339
  13.0 0.7 add_convert_fusion
  13.7 0.7 slice_bitcast_fusion
  14.4 3.0 %copy.18 = bf16[5120,256]{0,1:T(8,128)(2,1)S(1)} copy(bf16[5120,256]{1,0:T(8,128)(2,1)} %param.20) | data formatting | bytes 5242880 | tf_op args[4]
  17.4 0.0 copy-done.9
  17.4 0.0 copy-done.10
  17.5 0.0 copy-done.11
  17.5 0.1 concatenate.9.own
  17.6 0.1 fusion
  17.7 0.1 pad_maximum_fusion
  17.8 3.3 %all-to-all-done.recv = f32[16,4,640]{2,1,0:T(4,128)S(1)} async-done(((f32[16,4,640]{2,1,0:T(4,128)}), f32[16,4,640]{2,1,0:T(4,128)S(1)}, u32[]{:S(2)}, u32[]{:S(2)}) %all-to-all-start) | async-done | bytes 163872 | tf_op jit(solution)/shard_map/all_to_all | solution.py:339
  21.0 0.1 regroup.1
  21.2 21.9 %all_to_all.35.recv = f32[16,4,3456]{2,1,0:T(4,128)S(1)} all-to-all(f32[16,4,3456]{2,1,0:T(4,128)S(1)} %get-tuple-element.20), channel_id=1, replica_groups=mesh['group'=16,'tensor'=16] {'group'}, dimensions={0} | all-to-all | bytes 1769472 | tf_op jit(solution)/shard_map/all_to_all | solution.py:339
  43.1 0.2 assemble.1
  43.3 5.2 %all_to_all.36.recv = f32[2,64,3456]{2,1,0:T(8,128)S(1)} all-to-all(f32[2,64,3456]{2,1,0:T(8,128)S(1)} %assemble.1), channel_id=1, replica_groups={{0,16},{32,48},{64,80},{96,112},{128,144},{160,176},{192,208},{224,240}..., dimensions={0} | all-to-all | bytes 3538944 | tf_op jit(solution)/shard_map/all_to_all | solution.py:424
  48.5 0.0 copy-done.3
  48.5 0.0 copy-done.4
  48.5 0.0 copy-done.7
  48.5 2.7 %merge_queries.1 = (bf16[16,40,128]{2,1,0:T(8,128)(2,1)S(1)}, f32[64,256]{1,0:T(8,128)S(1)}, f32[64,320]{1,0:T(8,128)S(1)}, f32[2,64,128]{2,1,0:T(8,128)S(1)}) custom-call(f32[2,64,3456]{2,1,0:T(8,128)S(1)} %all_to_all.36.recv, bf16[256,5120]{1,0:T(8,128)(2,1)S(1)} %bitcast.13, bf16[16,5120]{1,0:T(8,128)(2,1)S(1)} %copy-done.3, f32[16,320]{1,0:T(8,128)S(1)} %copy-done.4, ...), custom_call_target="tpu_custom_call" | custom-call | tf_op jit(solution)/shard_map/merge_queries/pallas_call | solution.py:48
  51.3 0.0 copy-start
  51.3 13.4 %all_to_all.37.recv = bf16[16,40,128]{2,1,0:T(8,128)(2,1)S(1)} all-to-all(bf16[16,40,128]{2,1,0:T(8,128)(2,1)S(1)} %get-tuple-element.26), channel_id=1, replica_groups={{0,4,8,12,2,6,10,14,1,5,9,13,3,7,11,15},{16,20,24,28,18,22,26,30,17,21,..., dimensions={0} | all-to-all | bytes 327680 | tf_op jit(solution)/shard_map/all_to_all | solution.py:339
  64.7 0.0 copy-done.1
  64.7 0.0 copy-done.2
  64.7 0.0 copy-done.8
  64.7 1.8 %attend.1 = bf16[16,40,128]{2,1,0:T(8,128)(2,1)S(1)} custom-call(s32[4]{0:T(128)S(1)} %copy-done.8, bf16[16,40,128]{2,1,0:T(8,128)(2,1)S(1)} %all_to_all.37.recv, bf16[4,256,512]{2,1,0:T(8,128)(2,1)S(1)} %copy-done.1, bf16[4,256,512]{2,1,0:T(8,128)(2,1)S(1)} %copy-done.2, f32[4,256]{1,0:T(4,128)S(1)} %get-tuple-element.27.base, ...), custom_call_target="tpu_custom_call" | custom-call | tf_op jit(solution)/shard_map/attend/pallas_call | solution.py:48
  66.5 12.3 %all_to_all.38.recv = bf16[16,40,128]{2,1,0:T(8,128)(2,1)S(1)} all-to-all(bf16[16,40,128]{2,1,0:T(8,128)(2,1)S(1)} %attend.1), channel_id=1, replica_groups={{0,4,8,12,2,6,10,14,1,5,9,13,3,7,11,15},{16,20,24,28,18,22,26,30,17,21,..., dimensions={0} | all-to-all | bytes 327680 | tf_op jit(solution)/shard_map/all_to_all | solution.py:339
  78.8 0.9 project.1
  79.7 12.3 %all_to_all.39.recv = bf16[16,16,384]{2,1,0:T(8,128)(2,1)S(1)} all-to-all(bf16[16,16,384]{2,1,0:T(8,128)(2,1)S(1)} %project.1), channel_id=1, replica_groups={{0,4,8,12,2,6,10,14,1,5,9,13,3,7,11,15},{16,20,24,28,18,22,26,30,17,21,..., dimensions={0} | all-to-all | bytes 393216 | tf_op jit(solution)/shard_map/all_to_all | solution.py:339
  91.9 0.3 add_residual.1
  92.2 12.1 %all_to_all.40.recv = bf16[16,40,128]{2,1,0:T(8,128)(2,1)S(1)} all-to-all(bf16[16,40,128]{2,1,0:T(8,128)(2,1)S(1)} %add_residual.1), channel_id=1, replica_groups={{0,4,8,12,2,6,10,14,1,5,9,13,3,7,11,15},{16,20,24,28,18,22,26,30,17,21,..., dimensions={0} | all-to-all | bytes 327680 | tf_op jit(solution)/shard_map/all_to_all | solution.py:339
  104.4 1.0 finish.1
  (16 shorter events, 0.0 us)
Async XLA Ops:
  3.0 18.1 %all-to-all-start = ((f32[16,4,640]{2,1,0:T(4,128)}), f32[16,4,640]{2,1,0:T(4,128)S(1)}, u32[]{:S(2)}, u32[]{:S(2)}) async-start(f32[16,4,640]{2,1,0:T(4,128)} %get-tuple-element.17), calls=%async_computation | async-start | bytes 327680 | tf_op jit(solution)/shard_map/all_to_all | solution.py:339
  14.4 3.0 %copy-start.9 = (f32[4,320]{1,0:T(4,128)S(1)}, f32[4,320]{1,0:T(4,128)}, u32[]{:S(2)}) copy-start(f32[4,320]{1,0:T(4,128)} %param.28) | copy-start | bytes 15364
  14.4 3.1 %copy-start.10 = (f32[4,256]{1,0:T(4,128)S(1)}, f32[4,256]{1,0:T(4,128)}, u32[]{:S(2)}) copy-start(f32[4,256]{1,0:T(4,128)} %param.24) | copy-start | bytes 12292
  14.4 3.1 %copy-start.11 = (f32[256,4]{0,1:T(4,128)S(1)}, f32[256,4]{0,1:T(4,128)}, u32[]{:S(2)}) copy-start(f32[256,4]{0,1:T(4,128)} %param.27) | copy-start | bytes 12292
  43.1 5.4 %copy-start.3 = (bf16[16,5120]{1,0:T(8,128)(2,1)S(1)}, bf16[16,5120]{1,0:T(8,128)(2,1)}, u32[]{:S(2)}) copy-start(bf16[16,5120]{1,0:T(8,128)(2,1)} %get-tuple-element.22.x) | copy-start | bytes 491524
  43.1 5.4 %copy-start.4 = (f32[16,320]{1,0:T(8,128)S(1)}, f32[16,320]{1,0:T(8,128)}, u32[]{:S(2)}) copy-start(f32[16,320]{1,0:T(8,128)} %get-tuple-element.23.xt) | copy-start | bytes 61444
  43.1 5.4 %copy-start.7 = (f32[2,128]{1,0:T(2,128)S(1)}, f32[2,128]{1,0:T(2,128)}, u32[]{:S(2)}) copy-start(f32[2,128]{1,0:T(2,128)} %gains.3) | copy-start | bytes 3076
  48.5 16.2 %copy-start.1 = (bf16[4,256,512]{2,1,0:T(8,128)(2,1)S(1)}, bf16[4,256,512]{2,1,0:T(8,128)(2,1)}, u32[]{:S(2)}) copy-start(bf16[4,256,512]{2,1,0:T(8,128)(2,1)} %ck.1) | copy-start | bytes 3145732
  48.5 16.2 %copy-start.2 = (bf16[4,256,512]{2,1,0:T(8,128)(2,1)S(1)}, bf16[4,256,512]{2,1,0:T(8,128)(2,1)}, u32[]{:S(2)}) copy-start(bf16[4,256,512]{2,1,0:T(8,128)(2,1)} %cv.1) | copy-start | bytes 3145732
  48.5 16.2 %copy-start.8 = (s32[4]{0:T(128)S(1)}, s32[4]{0:T(128)}, u32[]{:S(2)}) copy-start(s32[4]{0:T(128)} %lengths.1) | copy-start | bytes 52
  51.3 27.5 %copy-start = (bf16[256,5120]{1,0:T(8,128)(2,1)S(1)}, bf16[256,5120]{1,0:T(8,128)(2,1)}, u32[]{:S(2)}) copy-start(bf16[256,5120]{1,0:T(8,128)(2,1)} %ow.1) | copy-start | bytes 7864324
  64.7 27.2 %copy-start.5 = (f32[16,320]{1,0:T(8,128)S(1)}, f32[16,320]{1,0:T(8,128)}, u32[]{:S(2)}) copy-start(f32[16,320]{1,0:T(8,128)} %get-tuple-element.31.st) | copy-start | bytes 61444
  66.5 37.9 %copy-start.6 = (bf16[5120]{0:T(1024)(128)(2,1)S(1)}, bf16[5120]{0:T(1024)(128)(2,1)}, u32[]{:S(2)}) copy-start(bf16[5120]{0:T(1024)(128)(2,1)} %param.18) | copy-start | bytes 30724
